TPU v7x, 32 devices: a whole 2x2x4 slice. The times are simulated.
32 devices in a mesh: section: 2 (over x), fsdp: 4 (over y, core), tp: 4 (over z).
Axes of the slice: x: 2, y: 2, z: 4, core: 2. Of those that a mesh axis runs over, the one named last changes fastest.
Arguments:
- queries: bfloat16 [2, 512, 4096], P('section', 'fsdp', 'tp'), may hold values from -160 to 160
- key_rows: bfloat16 [2, 512, 512], P('section', 'fsdp', 'tp'), may hold values from -8 to 8
- values: bfloat16 [2, 512, 512], P('section', 'fsdp', 'tp'), may hold values from -6 to 6
- segments: int32 [2, 512], P('section', 'fsdp'), may hold values from 0 to 3, never falling along the last dimension, each value on 1 to 384 neighbouring positions
- held_queries: bfloat16 [2, 512, 4096], P('section', ('fsdp', 'tp')), may hold values from -160 to 160
- held_keys: bfloat16 [2, 512, 512], P('section', ('fsdp', 'tp')), may hold values from -8 to 8
- held_values: bfloat16 [2, 512, 512], P('section', ('fsdp', 'tp')), may hold values from -6 to 6
- held_segments: int32 [2, 512], P('section', 'fsdp'), may hold values from 0 to 3, never falling along the last dimension, each value on 1 to 384 neighbouring positions
- out_grad: bfloat16 [2, 512, 4096], P('section', 'fsdp', 'tp'), may hold values from -6 to 6
Outputs:
- attn_out: bfloat16 [2, 512, 4096], P('section', 'fsdp', 'tp')
- query_grad: bfloat16 [2, 512, 4096], P('section', 'fsdp', 'tp')
- key_grad: bfloat16 [2, 512, 512], P('section', 'fsdp', 'tp')
- value_grad: bfloat16 [2, 512, 512], P('section', 'fsdp', 'tp')
All inputs are finite; a program needn't handle non-finite values.
Results may differ from a plain program's by a relative error of at most 0.014.
Values may be sent and summed in bfloat16 or wider, within the bound.
A program may use at most 64 MiB of HBM per device.

v0:
```python
import math

import jax
import jax.numpy as jnp
from jax import lax
from jax.sharding import PartitionSpec as P

HEAD_DIM = 128


NEG = -1e30


def partner(block, axis, apart):
    count = lax.axis_size(axis)
    route = []
    for low in range(count):
        high = low | 1 << apart
        if high != low and high < count:
            route += [(low, high), (high, low)]
    return lax.ppermute(block, axis, route)


def head_split(flat, group_count):
    return flat.reshape(flat.shape[0], group_count, -1, HEAD_DIM)


def visible_pairs(query_pos, query_seg, key_pos, key_seg):
    return (key_pos[None, :] <= query_pos[:, None]) & (key_seg[None, :] == query_seg[:, None])


def online_update(state_carry, query_heads, key_block, value_block, visible):
    running_max, running_sum, accumulated = state_carry
    scores = jnp.einsum(
        "igrd,jgd->igrj", query_heads, key_block, preferred_element_type=jnp.float32
    ) * (1.0 / math.sqrt(HEAD_DIM))
    visible_wide = visible[:, None, None, :]
    scores = jnp.where(visible_wide, scores, NEG)
    new_max = jnp.maximum(running_max, jnp.max(scores, axis=-1))
    weights = jnp.where(visible_wide, jnp.exp(scores - new_max[..., None]), 0.0)
    rescale = jnp.exp(running_max - new_max)
    running_sum = running_sum * rescale + jnp.sum(weights, axis=-1)
    accumulated = accumulated * rescale[..., None] + jnp.einsum(
        "igrj,jgd->igrd",
        weights.astype(jnp.bfloat16),
        value_block,
        preferred_element_type=jnp.float32,
    )
    return (new_max, running_sum, accumulated)


def attend(state_carry, query_heads, visible, key_block, value_block):
    return online_update(state_carry, query_heads, key_block, value_block, visible)


def block_grads(query_heads, grad_heads, log_total, delta_rows, visible, key_block, value_block):
    scores = jnp.einsum(
        "igrd,jgd->igrj", query_heads, key_block, preferred_element_type=jnp.float32
    ) * (1.0 / math.sqrt(HEAD_DIM))
    probabilities = jnp.where(
        visible[:, None, None, :], jnp.exp(scores - log_total[..., None]), 0.0
    )
    value_part = jnp.einsum(
        "igrj,igrd->jgd",
        probabilities.astype(jnp.bfloat16),
        grad_heads,
        preferred_element_type=jnp.float32,
    )
    prob_grad = jnp.einsum(
        "igrd,jgd->igrj", grad_heads, value_block, preferred_element_type=jnp.float32
    )
    score_grad = (probabilities * (prob_grad - delta_rows[..., None])).astype(jnp.bfloat16)
    query_part = jnp.einsum(
        "igrj,jgd->igrd", score_grad, key_block, preferred_element_type=jnp.float32
    )
    key_part = jnp.einsum(
        "igrj,igrd->jgd", score_grad, query_heads, preferred_element_type=jnp.float32
    )
    return (query_part, key_part, value_part)


def masked_grads(query_heads, grad_heads, log_total, delta_rows, visible, key_block, value_block):
    return block_grads(
        query_heads, grad_heads, log_total, delta_rows, visible, key_block, value_block
    )


def local(
    queries,
    key_rows,
    values,
    segments,
    held_queries,
    held_keys,
    held_values,
    held_segments,
    out_grad,
):
    row_count = queries.shape[1]
    group_count = key_rows.shape[2] // HEAD_DIM
    group_ratio = queries.shape[2] // key_rows.shape[2]
    score_scale = 1.0 / math.sqrt(HEAD_DIM)
    own_pos = lax.axis_index("fsdp") * row_count + jnp.arange(row_count, dtype=jnp.int32)
    blank_state = (
        jnp.full((row_count, group_count, group_ratio), NEG, jnp.float32),
        jnp.zeros((row_count, group_count, group_ratio), jnp.float32),
        jnp.zeros((row_count, group_count, group_ratio, HEAD_DIM), jnp.float32),
    )
    fwd_query = head_split(queries[0], group_count)
    fwd_seg = segments[0]
    key_piece = lax.all_gather(key_rows[0], "fsdp", axis=0, tiled=True)
    value_piece = lax.all_gather(values[0], "fsdp", axis=0, tiled=True)
    seg_piece = lax.all_gather(segments[0], "fsdp", axis=0, tiled=True)
    piece_rows = key_piece.shape[0]
    key_pos = jnp.arange(piece_rows, dtype=jnp.int32)
    visible = visible_pairs(own_pos, fwd_seg, key_pos, seg_piece)
    forward_state = attend(
        blank_state,
        fwd_query,
        visible,
        key_piece.reshape(piece_rows, group_count, HEAD_DIM),
        value_piece.reshape(piece_rows, group_count, HEAD_DIM),
    )
    attn_out = (
        (forward_state[2] / forward_state[1][..., None])
        .astype(jnp.bfloat16)
        .reshape(row_count, -1)[None]
    )
    bit_total = lax.axis_size("section").bit_length() - 1
    stash_items = (held_queries, held_keys, held_values, held_segments)
    for bit_index in range(bit_total):
        stash_items = partner(
            (stash_items[0], stash_items[1], stash_items[2], stash_items[3]), "section", bit_index
        )
    stash_query = stash_items[0][0]
    stash_key = stash_items[1][0]
    stash_value = stash_items[2][0]
    back_seg = stash_items[3][0]
    back_query, back_key, back_value = (
        lax.all_to_all(stash_query, "tp", split_axis=1, concat_axis=0, tiled=True),
        lax.all_to_all(stash_key, "tp", split_axis=1, concat_axis=0, tiled=True),
        lax.all_to_all(stash_value, "tp", split_axis=1, concat_axis=0, tiled=True),
    )
    full_key, full_value, full_seg = (
        lax.all_gather(back_key, "fsdp", axis=0, tiled=True),
        lax.all_gather(back_value, "fsdp", axis=0, tiled=True),
        lax.all_gather(back_seg, "fsdp", axis=0, tiled=True),
    )
    seq_len = full_key.shape[0]
    block_rows = min(512, seq_len)
    block_count = seq_len // block_rows
    key_blocks = full_key.reshape(block_count, block_rows, group_count, HEAD_DIM)
    value_blocks = full_value.reshape(block_count, block_rows, group_count, HEAD_DIM)
    seg_blocks = full_seg.reshape(block_count, block_rows)
    pos_blocks = jnp.arange(seq_len, dtype=jnp.int32).reshape(block_count, block_rows)
    back_heads = head_split(back_query, group_count)
    grad_heads = head_split(out_grad[0], group_count)

    def recompute_step(state_carry, block_items):
        key_block, value_block, seg_block, pos_block = block_items
        visible = visible_pairs(own_pos, back_seg, pos_block, seg_block)
        return (attend(state_carry, back_heads, visible, key_block, value_block), None)

    back_state, unused_output = lax.scan(
        recompute_step, blank_state, (key_blocks, value_blocks, seg_blocks, pos_blocks)
    )
    running_max, running_sum, accumulated = back_state
    log_total = running_max + jnp.log(running_sum)
    delta_rows = jnp.sum(
        grad_heads.astype(jnp.float32) * (accumulated / running_sum[..., None]), axis=-1
    )

    def key_block_step(query_sum, block_items):
        key_block, value_block, seg_block, pos_block = block_items
        visible = visible_pairs(own_pos, back_seg, pos_block, seg_block)
        query_part, key_part, value_part = masked_grads(
            back_heads, grad_heads, log_total, delta_rows, visible, key_block, value_block
        )
        return (query_sum + query_part, (key_part, value_part))

    query_zero = jnp.zeros((row_count, group_count, group_ratio, HEAD_DIM), jnp.float32)
    query_total, block_parts = lax.scan(
        key_block_step, query_zero, (key_blocks, value_blocks, seg_blocks, pos_blocks)
    )
    key_parts, value_parts = block_parts
    key_sums, value_sums = (
        lax.psum_scatter(
            key_parts.reshape(seq_len, -1).astype(jnp.bfloat16),
            "fsdp",
            scatter_dimension=0,
            tiled=True,
        ).astype(jnp.float32),
        lax.psum_scatter(
            value_parts.reshape(seq_len, -1).astype(jnp.bfloat16),
            "fsdp",
            scatter_dimension=0,
            tiled=True,
        ).astype(jnp.float32),
    )
    query_grad = (query_total * score_scale).astype(jnp.bfloat16).reshape(row_count, -1)[None]
    key_grad = (key_sums * score_scale).astype(jnp.bfloat16)[None]
    value_grad = value_sums.astype(jnp.bfloat16)[None]
    return (attn_out, query_grad, key_grad, value_grad)


def solution(mesh):
    return jax.shard_map(
        local,
        mesh=mesh,
        in_specs=(
            P("section", "fsdp", "tp"),
            P("section", "fsdp", "tp"),
            P("section", "fsdp", "tp"),
            P("section", "fsdp"),
            P("section", ("fsdp", "tp"), None),
            P("section", ("fsdp", "tp"), None),
            P("section", ("fsdp", "tp"), None),
            P("section", "fsdp"),
            P("section", "fsdp", "tp"),
        ),
        out_specs=(
            P("section", "fsdp", "tp"),
            P("section", "fsdp", "tp"),
            P("section", "fsdp", "tp"),
            P("section", "fsdp", "tp"),
        ),
        check_vma=False,
    )
```

profile of v0, /device:TPU:1, one launch (start us, length us, event | category | flops | bytes accessed | tf_op | source)
XLA Modules:
  0.0 130.2 jit_solution(4046799372539779245)
XLA Ops:
  7.2 0.0 copy-start.1
  7.2 2.1 %collective-permute-start = (s32[1,128]{1,0:T(1,128)}, s32[1,128]{1,0:T(1,128)S(1)}, u32[]{:S(2)}, u32[]{:S(2)}) collective-permute-start(s32[1,128]{1,0:T(1,128)} %param.16), channel_id=1, source_target_pairs={{0,16},{16,0},{1,17},{17,1},{2,18},{18,2},{3,19},{19,3},{4,20},{20... | collective-permute-start | bytes 1544 | tf_op jit(solution)/shard_map/ppermute | solution.py:21
  9.3 0.1 collective-permute-start.1
  9.4 1.4 %collective-permute-start.3 = (bf16[1,32,512]{2,1,0:T(8,128)(2,1)}, bf16[1,32,512]{2,1,0:T(8,128)(2,1)S(1)}, u32[]{:S(2)}, u32[]{:S(2)}) collective-permute-start(bf16[1,32,512]{2,1,0:T(8,128)(2,1)} %param.15), channel_id=1, source_target_pairs={{0,16},{16,0},{1,17},{17,1},{2,18},{18,2},{3,19},{19,3},{4,20},{20... | collective-permute-start | bytes 98312 | tf_op jit(solution)/shard_map/ppermute | solution.py:21
  10.7 0.1 collective-permute-start.2
  10.8 0.9 copy.28
  11.7 6.9 %all-gather.2 = bf16[1,512,128]{1,2,0:T(8,128)(2,1)S(1)} all-gather(bf16[1,128,128]{1,2,0:T(8,128)(2,1)S(1)} %copy.28), channel_id=4, replica_groups=mesh['section'=2,'fsdp'=4,'tp'=4] {'fsdp'}, dimensions={1}, use_global_device_ids=true | all-gather | bytes 163840 | tf_op jit(solution)/shard_map/all_gather | solution.py:112
  18.6 5.8 %all-gather.1 = bf16[1,512,128]{2,1,0:T(8,128)(2,1)S(1)} all-gather(bf16[1,128,128]{2,1,0:T(8,128)(2,1)} %param.10), channel_id=3, replica_groups=mesh['section'=2,'fsdp'=4,'tp'=4] {'fsdp'}, dimensions={1}, use_global_device_ids=true | all-gather | bytes 163840 | tf_op jit(solution)/shard_map/all_gather | solution.py:111
  24.4 1.0 copy.51
  25.4 1.1 copy.35
  26.5 1.7 %copy.53 = bf16[16,8,8,128]{3,2,1,0:T(8,128)(2,1)} copy(bf16[16,8,8,128]{3,1,2,0:T(8,128)(2,1)} %bitcast.165) | data formatting | bytes 524288
  28.2 0.0 copy-done.1
  28.2 5.0 %all-gather = s32[1,512]{1,0:T(1,128)S(1)} all-gather(s32[1,128]{1,0:T(1,128)S(1)} %copy-done.1), channel_id=2, replica_groups=mesh['section'=2,'fsdp'=4,'tp'=4] {'fsdp'}, dimensions={1}, use_global_device_ids=true | all-gather | bytes 2560 | tf_op jit(solution)/shard_map/all_gather | solution.py:113
  33.2 0.0 collective-permute-done
  33.2 5.0 %all-gather.3 = s32[1,512]{1,0:T(1,128)S(1)} all-gather(s32[1,128]{1,0:T(1,128)S(1)} %collective-permute-done), channel_id=5, replica_groups=mesh['section'=2,'fsdp'=4,'tp'=4] {'fsdp'}, dimensions={1}, use_global_device_ids=true | all-gather | bytes 2560 | tf_op jit(solution)/shard_map/all_gather | solution.py:147
  38.2 0.2 fusion.44
  38.4 0.5 fusion.4
  38.9 0.0 collective-permute-done.1
  38.9 0.6 copy.30
  39.5 4.8 %all-to-all-start = ((bf16[32,4,128]{2,0,1:T(8,128)(2,1)}), bf16[32,4,128]{2,0,1:T(8,128)(2,1)S(1)}, u32[]{:S(2)}, u32[]{:S(2)}) async-start(bf16[32,4,128]{2,0,1:T(8,128)(2,1)} %copy.30), calls=%async_computation | async-start | bytes 65536 | tf_op jit(solution)/shard_map/all_to_all | solution.py:141
  44.3 0.5 fusion.6
  44.8 0.0 collective-permute-done.3
  44.9 0.6 copy.33
  45.5 3.3 %all-to-all-done = bf16[32,4,128]{2,0,1:T(8,128)(2,1)S(1)} async-done(((bf16[32,4,128]{2,0,1:T(8,128)(2,1)}), bf16[32,4,128]{2,0,1:T(8,128)(2,1)S(1)}, u32[]{:S(2)}, u32[]{:S(2)}) %all-to-all-start) | async-done | bytes 32800 | tf_op jit(solution)/shard_map/all_to_all | solution.py:141
  48.8 3.3 %all-to-all-start.2 = ((bf16[32,4,128]{2,0,1:T(8,128)(2,1)}), bf16[32,4,128]{2,0,1:T(8,128)(2,1)S(1)}, u32[]{:S(2)}, u32[]{:S(2)}) async-start(bf16[32,4,128]{2,0,1:T(8,128)(2,1)} %copy.33), calls=%async_computation.2 | async-start | bytes 65536 | tf_op jit(solution)/shard_map/all_to_all | solution.py:142
  52.1 0.0 collective-permute-done.2
  52.1 1.1 all_to_all.44
  53.2 0.8 copy.31
  54.0 2.5 %all-to-all-done.2 = bf16[32,4,128]{2,0,1:T(8,128)(2,1)S(1)} async-done(((bf16[32,4,128]{2,0,1:T(8,128)(2,1)}), bf16[32,4,128]{2,0,1:T(8,128)(2,1)S(1)}, u32[]{:S(2)}, u32[]{:S(2)}) %all-to-all-start.2) | async-done | bytes 32800 | tf_op jit(solution)/shard_map/all_to_all | solution.py:142
  56.6 3.4 %all-to-all-start.1 = ((bf16[32,4,1024]{2,0,1:T(8,128)(2,1)}), bf16[32,4,1024]{2,0,1:T(8,128)(2,1)S(1)}, u32[]{:S(2)}, u32[]{:S(2)}) async-start(bf16[32,4,1024]{2,0,1:T(8,128)(2,1)} %copy.31), calls=%async_computation.1 | async-start | bytes 524288 | tf_op jit(solution)/shard_map/all_to_all | solution.py:140
  60.0 0.0 reduce-scatter.3.cloned.1.call-start
  60.0 1.4 %fusion.17 = bf16[1,128,128,8]{2,1,3,0:T(8,128)(2,1)} fusion(f32[512,128,8]{1,0,2:T(8,128)S(1)} %get-tuple-element.81, f32[128,8]{0,1:T(8,128)S(1)} %broadcast_maximum_fusion.1, pred[128,512]{0,1:T(8,128)(4,1)S(1)} %get-tuple-element.79, f32[128,8]{0,1:T(8,128)S(1)} %get-tuple-element.77, f32[128,8]{0,1:T(8,128)S(1)} %get-tuple-element.76, ...), kind=kOutput, calls=%fused_computation.27 | convolution fusion | flops 137232384 | bytes 2568192 | tf_op jit(solution)/shard_map/igrj,jgd->igrd/dot_general | solution.py:43
  61.4 1.8 %copy.42 = bf16[1,128,1024]{2,1,0:T(8,128)(2,1)} copy(bf16[1,128,1024]{1,2,0:T(8,128)(2,1)} %bitcast.175) | data formatting | bytes 524288
  63.2 8.0 %all_gather.23 = bf16[512,128]{1,0:T(8,128)(2,1)S(1)} all-gather(bf16[128,128]{1,0:T(8,128)(2,1)S(1)} %bitcast.177), channel_id=1, replica_groups=mesh['section'=2,'fsdp'=4,'tp'=4] {'fsdp'}, dimensions={0}, use_global_device_ids=true | all-gather | bytes 163840 | tf_op jit(solution)/shard_map/all_gather | solution.py:146
  71.2 5.4 %all_gather.22 = bf16[512,128]{1,0:T(8,128)(2,1)S(1)} all-gather(bf16[128,128]{1,0:T(8,128)(2,1)S(1)} %bitcast.176), channel_id=1, replica_groups=mesh['section'=2,'fsdp'=4,'tp'=4] {'fsdp'}, dimensions={0}, use_global_device_ids=true | all-gather | bytes 163840 | tf_op jit(solution)/shard_map/all_gather | solution.py:145
  76.6 0.0 all-to-all-done.1
  76.7 0.4 fusion.3
  77.1 0.5 fusion.9
  77.7 0.0 copy-start
  77.7 0.6 fusion.19
  78.3 0.3 copy-done
  78.6 0.7 fusion.10
  79.4 1.1 fusion.20
  80.5 0.0 reduce-scatter.3.cloned.1.call-update
  80.5 0.0 reduce-scatter.5.cloned.1.call-start
  80.6 2.1 %fusion.21 = bf16[512,128]{1,0:T(8,128)(2,1)} fusion(f32[512,128,8]{1,0,2:T(8,128)S(1)} %get-tuple-element.83, f32[128,8]{0,1:T(8,128)S(1)} %get-tuple-element.73, pred[128,512]{0,1:T(8,128)(4,1)S(1)} %get-tuple-element.78, bf16[128,8,128]{2,1,0:T(8,128)(2,1)} %bitcast.173), kind=kOutput, calls=%fused_computation.33 | convolution fusion | flops 136380416 | bytes 2560000 | tf_op jit(solution)/shard_map/while/body/eval_jaxpr/igrj,igrd->jgd/dot_general | solution.py:63
  82.7 0.0 reduce-scatter.5.cloned.1.call-update
  82.7 0.4 fusion.18
  83.0 0.9 copy.43
  83.9 16.7 %reduce-scatter.3.cloned.1.call-done = bf16[128,128]{1,0:T(8,128)(2,1)} async-done(((bf16[512,128]{1,0:T(8,128)(2,1)}), bf16[128,128]{1,0:T(8,128)(2,1)}) %reduce-scatter.3.cloned.1.call-update) | async-done | bytes 32784 | tf_op jit(solution)/shard_map/reduce_scatter | solution.py:187
  100.6 1.4 %fusion.57 = bf16[1,128,128]{2,1,0:T(8,128)(2,1)} fusion(bf16[128,128]{1,0:T(8,128)(2,1)} %reduce-scatter.3.cloned.1.call-done), kind=kLoop, calls=%fused_computation.68 | loop fusion | flops 49152 | bytes 65536 | tf_op jit(solution)/shard_map/broadcast_in_dim | solution.py:201
  102.0 21.4 %reduce-scatter.5.cloned.1.call-done = bf16[128,128]{1,0:T(8,128)(2,1)} async-done(((bf16[512,128]{1,0:T(8,128)(2,1)}), bf16[128,128]{1,0:T(8,128)(2,1)}) %reduce-scatter.5.cloned.1.call-update) | async-done | bytes 32784 | tf_op jit(solution)/shard_map/reduce_scatter | solution.py:193
  (8 shorter events, 0.1 us)
Async XLA Ops:
  7.2 21.0 %copy-start.1 = (s32[1,128]{1,0:T(1,128)S(1)}, s32[1,128]{1,0:T(1,128)}, u32[]{:S(2)}) copy-start(s32[1,128]{1,0:T(1,128)} %param.12) | copy-start | bytes 1540
  7.2 26.0 %collective-permute-start = (s32[1,128]{1,0:T(1,128)}, s32[1,128]{1,0:T(1,128)S(1)}, u32[]{:S(2)}, u32[]{:S(2)}) collective-permute-start(s32[1,128]{1,0:T(1,128)} %param.16), channel_id=1, source_target_pairs={{0,16},{16,0},{1,17},{17,1},{2,18},{18,2},{3,19},{19,3},{4,20},{20... | collective-permute-start | bytes 1544 | tf_op jit(solution)/shard_map/ppermute | solution.py:21
  9.3 29.6 %collective-permute-start.1 = (bf16[1,32,512]{2,1,0:T(8,128)(2,1)}, bf16[1,32,512]{2,1,0:T(8,128)(2,1)S(1)}, u32[]{:S(2)}, u32[]{:S(2)}) collective-permute-start(bf16[1,32,512]{2,1,0:T(8,128)(2,1)} %param.14), channel_id=1, source_target_pairs={{0,16},{16,0},{1,17},{17,1},{2,18},{18,2},{3,19},{19,3},{4,20},{20... | collective-permute-start | bytes 98312 | tf_op jit(solution)/shard_map/ppermute | solution.py:21
  9.4 35.5 %collective-permute-start.3 = (bf16[1,32,512]{2,1,0:T(8,128)(2,1)}, bf16[1,32,512]{2,1,0:T(8,128)(2,1)S(1)}, u32[]{:S(2)}, u32[]{:S(2)}) collective-permute-start(bf16[1,32,512]{2,1,0:T(8,128)(2,1)} %param.15), channel_id=1, source_target_pairs={{0,16},{16,0},{1,17},{17,1},{2,18},{18,2},{3,19},{19,3},{4,20},{20... | collective-permute-start | bytes 98312 | tf_op jit(solution)/shard_map/ppermute | solution.py:21
  10.7 41.4 %collective-permute-start.2 = (bf16[1,32,4096]{2,1,0:T(8,128)(2,1)}, bf16[1,32,4096]{2,1,0:T(8,128)(2,1)}, u32[]{:S(2)}, u32[]{:S(2)}) collective-permute-start(bf16[1,32,4096]{2,1,0:T(8,128)(2,1)} %param.13), channel_id=1, source_target_pairs={{0,16},{16,0},{1,17},{17,1},{2,18},{18,2},{3,19},{19,3},{4,20},{20... | collective-permute-start | bytes 786440 | tf_op jit(solution)/shard_map/ppermute | solution.py:21
  39.5 9.3 %all-to-all-start = ((bf16[32,4,128]{2,0,1:T(8,128)(2,1)}), bf16[32,4,128]{2,0,1:T(8,128)(2,1)S(1)}, u32[]{:S(2)}, u32[]{:S(2)}) async-start(bf16[32,4,128]{2,0,1:T(8,128)(2,1)} %copy.30), calls=%async_computation | async-start | bytes 65536 | tf_op jit(solution)/shard_map/all_to_all | solution.py:141
  48.8 7.7 %all-to-all-start.2 = ((bf16[32,4,128]{2,0,1:T(8,128)(2,1)}), bf16[32,4,128]{2,0,1:T(8,128)(2,1)S(1)}, u32[]{:S(2)}, u32[]{:S(2)}) async-start(bf16[32,4,128]{2,0,1:T(8,128)(2,1)} %copy.33), calls=%async_computation.2 | async-start | bytes 65536 | tf_op jit(solution)/shard_map/all_to_all | solution.py:142
  56.6 20.1 %all-to-all-start.1 = ((bf16[32,4,1024]{2,0,1:T(8,128)(2,1)}), bf16[32,4,1024]{2,0,1:T(8,128)(2,1)S(1)}, u32[]{:S(2)}, u32[]{:S(2)}) async-start(bf16[32,4,1024]{2,0,1:T(8,128)(2,1)} %copy.31), calls=%async_computation.1 | async-start | bytes 524288 | tf_op jit(solution)/shard_map/all_to_all | solution.py:140
  60.0 40.7 %reduce-scatter.3.cloned.1.call-start = ((), (), s32[]{:S(2)}) async-start(), calls=%async_computation.5 | async-start | bytes 163840 | tf_op jit(solution)/shard_map/reduce_scatter | solution.py:187
  77.7 1.0 copy-start
  80.5 42.9 %reduce-scatter.5.cloned.1.call-start = ((), (), s32[]{:S(2)}) async-start(), calls=%async_computation.6 | async-start | bytes 163840 | tf_op jit(solution)/shard_map/reduce_scatter | solution.py:193
Sparse Core Ops, SparseCore 0:
  80.6 19.9 reduce-scatter.2
  103.8 19.5 reduce-scatter.4
where the time goes:
time: 132 us; the launch traced here: 130 us
  waiting for transfers between devices  44 us (33%)
  blocking collectives  36.1 us (27%)
  starting transfers between devices  15.2 us (12%)
  between operations  14.2 us (11%)
  local copies, waits for them, and re-layouts  10.8 us (8%)
  matrix products  7.22 us (5%)
  other arithmetic  2.65 us (2%)
    reduce_scatter x1, waiting for transfers between devices, local(): lax.psum_scatter(value_parts.reshape(seq_len, -1).astype(jnp.bfloat16), '...  21.4 us
    reduce_scatter x1, waiting for transfers between devices, local(): lax.psum_scatter(key_parts.reshape(seq_len, -1).astype(jnp.bfloat16), 'fs...  16.7 us
    all_gather x1, blocking collectives, local(): lax.all_gather(back_value, 'fsdp', axis=0, tiled=True)  8.02 us
    all_gather x1, blocking collectives, local(): value_piece = lax.all_gather(values[0], 'fsdp', axis=0, tiled=True)  6.9 us
    unnamed x10, local copies, waits for them, and re-layouts  6.52 us
    all_gather x1, blocking collectives, local(): key_piece = lax.all_gather(key_rows[0], 'fsdp', axis=0, tiled=True)  5.79 us
    all_gather x1, blocking collectives, local(): lax.all_gather(back_key, 'fsdp', axis=0, tiled=True)  5.41 us
    all_gather x1, blocking collectives, local(): lax.all_gather(back_seg, 'fsdp', axis=0, tiled=True)  5.03 us
  transfers between devices with their start and end apart: 9, of which 4 were waited for; matrix products, arithmetic and copies ran while one was open for 12% of the time, Pallas kernels for 0%

commit v1 on v0

v1 whole, which is shorter than its diff:
```python
import functools
import math

import jax
import jax.numpy as jnp
from jax import lax
from jax.experimental import pallas as pl
from jax.experimental.pallas import tpu as pltpu
from jax.sharding import PartitionSpec as P

HEAD_DIM = 128
PAIR = 2
NEG = -1e30
SCALE = 1.0 / math.sqrt(HEAD_DIM)
SCALE_LOG2 = SCALE * math.log2(math.e)
MESH = pl.DeviceIdType.MESH

NT = (((1,), (1,)), ((), ()))


def dot(left, right, dims=(((1,), (0,)), ((), ()))):
    return lax.dot_general(left, right, dims, preferred_element_type=jnp.float32)


def kernel(
    n_s,
    n_f,
    n_t,
    q_ref,
    k_ref,
    v_ref,
    sg_ref,
    hq_ref,
    hk_ref,
    hv_ref,
    hs_ref,
    do_ref,
    o_ref,
    dq_ref,
    dk_ref,
    dv_ref,
    q_buf,
    g_buf,
    kv_fwd,
    sg_fwd,
    hq_buf,
    kv_held,
    sg_held,
    bias,
    turned,
    s_buf,
    p_buf,
    dk_acc,
    dv_acc,
    part_out,
    part_in,
    o_buf,
    dq_buf,
    dk_buf,
    dv_buf,
    local_sem,
    fwd_send,
    fwd_recv,
    one_send,
    one_recv,
    two_send,
    two_recv,
    hq_send,
    hq_recv,
    red_send,
    red_recv,
):
    rows = q_ref.shape[1]
    part_rows = hq_ref.shape[1]
    width = q_ref.shape[2]
    pair_width = PAIR * HEAD_DIM
    pairs = width // pair_width
    seq = n_f * rows
    block = min(512, seq)
    blocks = seq // block

    s, f, t = lax.axis_index("section"), lax.axis_index("fsdp"), lax.axis_index("tp")
    mirror = n_s - 1 - s

    def at_f(step):
        return lax.rem(f + step, n_f)

    def at_t(step):
        return lax.rem(t + step, n_t)

    local = [
        pltpu.make_async_copy(k_ref.at[0], kv_fwd.at[f, 0], local_sem.at[0]),
        pltpu.make_async_copy(v_ref.at[0], kv_fwd.at[f, 1], local_sem.at[1]),
        pltpu.make_async_copy(sg_ref, sg_fwd.at[f], local_sem.at[2]),
        pltpu.make_async_copy(q_ref.at[0], q_buf, local_sem.at[3]),
        pltpu.make_async_copy(do_ref.at[0], g_buf, local_sem.at[4]),
    ]
    for copy in local:
        copy.start()

    barrier = pltpu.get_barrier_semaphore()
    for step in range(n_t):
        pl.semaphore_signal(
            barrier, inc=1, device_id=(mirror, f, at_t(step)), device_id_type=MESH
        )
    for step in range(1, n_f):
        pl.semaphore_signal(barrier, inc=1, device_id=(s, at_f(step), t), device_id_type=MESH)
    pl.semaphore_wait(barrier, n_t + n_f - 1)

    def remote(src, dst, send_sem, recv_sem, device):
        return pltpu.make_async_remote_copy(
            src_ref=src,
            dst_ref=dst,
            send_sem=send_sem,
            recv_sem=recv_sem,
            device_id=device,
            device_id_type=MESH,
        )

    own_rows = pl.ds(pl.multiple_of(t * part_rows, part_rows), part_rows)

    first = []
    for step in range(n_t):
        to = at_t(step)
        columns = pl.ds(pl.multiple_of(to * HEAD_DIM, HEAD_DIM), HEAD_DIM)
        for which, held in enumerate((hk_ref, hv_ref)):
            first.append(
                remote(
                    held.at[0, :, columns],
                    kv_held.at[f, which, own_rows, :],
                    one_send.at[2 * step + which],
                    one_recv.at[2 * step + which],
                    (mirror, f, to),
                )
            )
    first.append(
        remote(
            hs_ref,
            sg_held.at[f],
            one_send.at[2 * n_t],
            one_recv.at[2 * n_t],
            (mirror, f, t),
        )
    )
    for copy in first:
        copy.start()

    fwd = []
    for step in range(1, n_f):
        device = (s, at_f(step), t)
        at = 3 * (step - 1)
        for which, src in enumerate((k_ref.at[0], v_ref.at[0], sg_ref)):
            dst = sg_fwd.at[f] if which == 2 else kv_fwd.at[f, which]
            fwd.append(
                remote(src, dst, fwd_send.at[at + which], fwd_recv.at[at + which], device)
            )
    for copy in fwd:
        copy.start()

    def query_copy(pair, step):
        to = at_t(step)
        columns = pl.ds(
            pl.multiple_of(to * width + pair * pair_width, pair_width), pair_width
        )
        return remote(
            hq_ref.at[0, :, columns],
            hq_buf.at[pair, own_rows, :],
            hq_send.at[pair, step],
            hq_recv.at[pair, step],
            (mirror, f, to),
        )

    for pair in range(pairs):
        for step in range(n_t):
            query_copy(pair, step).start()

    for copy in first:
        copy.wait_recv()
    second = []
    for step in range(1, n_f):
        device = (s, at_f(step), t)
        at = 2 * (step - 1)
        second.append(
            remote(
                kv_held.at[f], kv_held.at[f], two_send.at[at], two_recv.at[at], device
            )
        )
        second.append(
            remote(
                sg_held.at[f],
                sg_held.at[f],
                two_send.at[at + 1],
                two_recv.at[at + 1],
                device,
            )
        )
    for copy in second:
        copy.start()

    def make_bias(ids):
        own = ids[f]
        for b in range(n_f):
            key_ids = jnp.transpose(jnp.broadcast_to(ids[b], (HEAD_DIM, rows)))[:, :1]
            key_pos = b * rows + lax.broadcasted_iota(jnp.int32, (rows, rows), 0)
            own_pos = f * rows + lax.broadcasted_iota(jnp.int32, (rows, rows), 1)
            seen = (key_pos <= own_pos) & (key_ids == own)
            bias[b * rows : (b + 1) * rows, :] = jnp.where(seen, 0.0, NEG)

    def over_blocks(step, start):
        if blocks == 1:
            return step(0, start)
        return lax.fori_loop(0, blocks, step, start)

    def span(b):
        if blocks == 1:
            return pl.ds(0, block)
        return pl.ds(pl.multiple_of(b * block, block), block)

    def piece(kv, which, b):
        per = block // rows
        if blocks == 1:
            part = kv[:, which]
        else:
            part = kv[pl.ds(b * per, per), which]
        return part.reshape(block, HEAD_DIM)

    def turn(kv, which):
        for b in range(n_f):
            turned[:, b * rows : (b + 1) * rows] = jnp.transpose(kv[b, which])

    def stacked(pair_block):
        return jnp.concatenate(
            [pair_block[:, h * HEAD_DIM : (h + 1) * HEAD_DIM] for h in range(PAIR)], axis=0
        )

    def scores_of(kv, query):
        def step(b, top):
            masked = jnp.concatenate([bias[span(b), :]] * PAIR, axis=1)
            scores = dot(piece(kv, 0, b), query, NT) * SCALE_LOG2 + masked
            s_buf[span(b), :] = scores
            return jnp.maximum(top, jnp.max(scores, axis=0, keepdims=True))

        return over_blocks(step, jnp.full((1, PAIR * rows), NEG, jnp.float32))

    def untangled(wide):
        return jnp.concatenate(
            [
                jnp.transpose(wide[:, h * rows : (h + 1) * rows])
                for h in range(PAIR)
            ],
            axis=1,
        ).astype(jnp.bfloat16)

    def lanes_of(pair):
        return pl.ds(pl.multiple_of(pair * pair_width, pair_width), pair_width)

    for copy in local:
        copy.wait()
    for copy in fwd:
        copy.wait_recv()
    make_bias(sg_fwd)
    turn(kv_fwd, 1)

    def forward_pair(pair, carry):
        query = stacked(q_buf[:, lanes_of(pair)])
        top = scores_of(kv_fwd, query)

        def step(b, sums):
            total, out = sums
            weights = jnp.exp2(s_buf[span(b), :] - top)
            total = total + jnp.sum(weights, axis=0, keepdims=True)
            out = out + dot(turned[:, span(b)], weights.astype(jnp.bfloat16))
            return total, out

        total, out = over_blocks(
            step,
            (
                jnp.zeros((1, PAIR * rows), jnp.float32),
                jnp.zeros((HEAD_DIM, PAIR * rows), jnp.float32),
            ),
        )
        o_buf[:, lanes_of(pair)] = untangled(out * (1.0 / total))
        return carry

    lax.fori_loop(0, pairs, forward_pair, 0)
    out_copy = pltpu.make_async_copy(o_buf, o_ref.at[0], local_sem.at[0])
    out_copy.start()

    for copy in second:
        copy.wait_recv()
    make_bias(sg_held)
    turn(kv_held, 0)
    dk_acc[...] = jnp.zeros_like(dk_acc)
    dv_acc[...] = jnp.zeros_like(dv_acc)

    def backward_pair(pair, carry):
        for step in range(n_t):
            query_copy(pair, step).wait_recv()
        query = stacked(hq_buf[pair])
        grad = stacked(g_buf[:, lanes_of(pair)])
        top = scores_of(kv_held, query)

        def middle(b, sums):
            total, along = sums
            weights = jnp.exp2(s_buf[span(b), :] - top)
            prob_grad = dot(piece(kv_held, 1, b), grad, NT)
            s_buf[span(b), :] = weights
            p_buf[span(b), :] = prob_grad
            total = total + jnp.sum(weights, axis=0, keepdims=True)
            along = along + jnp.sum(weights * prob_grad, axis=0, keepdims=True)
            return total, along

        zero = jnp.zeros((1, PAIR * rows), jnp.float32)
        total, along = over_blocks(middle, (zero, zero))
        inverse = 1.0 / total
        delta = along * inverse

        def last(b, query_sum):
            probs = s_buf[span(b), :] * inverse
            score_grad = (probs * (p_buf[span(b), :] - delta)).astype(jnp.bfloat16)
            dv_acc[span(b), :] += dot(probs.astype(jnp.bfloat16), grad)
            dk_acc[span(b), :] += dot(score_grad, query)
            return query_sum + dot(turned[:, span(b)], score_grad)

        query_sum = over_blocks(last, jnp.zeros((HEAD_DIM, PAIR * rows), jnp.float32))
        dq_buf[:, lanes_of(pair)] = untangled(query_sum * SCALE)
        return carry

    lax.fori_loop(0, pairs, backward_pair, 0)
    query_grad_copy = pltpu.make_async_copy(dq_buf, dq_ref.at[0], local_sem.at[1])
    query_grad_copy.start()

    def rows_at(index):
        return pl.ds(pl.multiple_of(index * rows, rows), rows)

    reduce = []
    for step in range(1, n_f):
        to = at_f(step)
        part_out[step - 1, 0] = dk_acc[rows_at(to), :].astype(jnp.bfloat16)
        part_out[step - 1, 1] = dv_acc[rows_at(to), :].astype(jnp.bfloat16)
        copy = remote(
            part_out.at[step - 1],
            part_in.at[step - 1],
            red_send.at[step - 1],
            red_recv.at[step - 1],
            (s, to, t),
        )
        copy.start()
        reduce.append(copy)
    key_sum = dk_acc[rows_at(f), :]
    value_sum = dv_acc[rows_at(f), :]
    for step in range(1, n_f):
        reduce[step - 1].wait_recv()
        key_sum = key_sum + part_in[step - 1, 0].astype(jnp.float32)
        value_sum = value_sum + part_in[step - 1, 1].astype(jnp.float32)
    dk_buf[...] = (key_sum * SCALE).astype(jnp.bfloat16)
    dv_buf[...] = value_sum.astype(jnp.bfloat16)
    last_copies = [
        pltpu.make_async_copy(dk_buf, dk_ref.at[0], local_sem.at[2]),
        pltpu.make_async_copy(dv_buf, dv_ref.at[0], local_sem.at[3]),
    ]
    for copy in last_copies:
        copy.start()
    for copy in first + fwd + second + reduce:
        copy.wait_send()
    for pair in range(pairs):
        for step in range(n_t):
            query_copy(pair, step).wait_send()
    for copy in [out_copy, query_grad_copy] + last_copies:
        copy.wait()


def local(sizes, *arrays):
    n_s, n_f, n_t = sizes
    queries, key_rows = arrays[0], arrays[1]
    rows, width = queries.shape[1], queries.shape[2]
    pairs = width // (PAIR * HEAD_DIM)
    seq = n_f * rows
    low, full = jnp.bfloat16, jnp.float32
    dma = pltpu.SemaphoreType.DMA
    anywhere = pl.BlockSpec(memory_space=pl.ANY)
    elements = rows * (width // HEAD_DIM) * seq
    return pl.pallas_call(
        functools.partial(kernel, n_s, n_f, n_t),
        out_shape=[
            jax.ShapeDtypeStruct(queries.shape, low),
            jax.ShapeDtypeStruct(queries.shape, low),
            jax.ShapeDtypeStruct(key_rows.shape, low),
            jax.ShapeDtypeStruct(key_rows.shape, low),
        ],
        in_specs=[anywhere] * 9,
        out_specs=[anywhere] * 4,
        scratch_shapes=[
            pltpu.VMEM((rows, width), low),
            pltpu.VMEM((rows, width), low),
            pltpu.VMEM((n_f, 2, rows, HEAD_DIM), low),
            pltpu.VMEM((n_f, 1, rows), jnp.int32),
            pltpu.VMEM((pairs, rows, PAIR * HEAD_DIM), low),
            pltpu.VMEM((n_f, 2, rows, HEAD_DIM), low),
            pltpu.VMEM((n_f, 1, rows), jnp.int32),
            pltpu.VMEM((seq, rows), full),
            pltpu.VMEM((HEAD_DIM, seq), low),
            pltpu.VMEM((seq, PAIR * rows), full),
            pltpu.VMEM((seq, PAIR * rows), full),
            pltpu.VMEM((seq, HEAD_DIM), full),
            pltpu.VMEM((seq, HEAD_DIM), full),
            pltpu.VMEM((n_f - 1, 2, rows, HEAD_DIM), low),
            pltpu.VMEM((n_f - 1, 2, rows, HEAD_DIM), low),
            pltpu.VMEM((rows, width), low),
            pltpu.VMEM((rows, width), low),
            pltpu.VMEM((rows, HEAD_DIM), low),
            pltpu.VMEM((rows, HEAD_DIM), low),
            dma((5,)),
            dma((3 * (n_f - 1),)),
            dma((3 * (n_f - 1),)),
            dma((2 * n_t + 1,)),
            dma((2 * n_t + 1,)),
            dma((2 * (n_f - 1),)),
            dma((2 * (n_f - 1),)),
            dma((pairs, n_t)),
            dma((pairs, n_t)),
            dma((n_f - 1,)),
            dma((n_f - 1,)),
        ],
        compiler_params=pltpu.CompilerParams(
            collective_id=0, has_side_effects=True, vmem_limit_bytes=40 * 1024 * 1024
        ),
        cost_estimate=pl.CostEstimate(
            flops=14 * elements * HEAD_DIM,
            bytes_accessed=6 * rows * width * 2,
            transcendentals=2 * elements,
        ),
        name="tick",
    )(*arrays)


def solution(mesh):
    sizes = (mesh.shape["section"], mesh.shape["fsdp"], mesh.shape["tp"])
    by_head = P("section", "fsdp", "tp")
    by_row = P("section", ("fsdp", "tp"), None)
    ids = P("section", "fsdp")
    return jax.shard_map(
        functools.partial(local, sizes),
        mesh=mesh,
        in_specs=(by_head, by_head, by_head, ids, by_row, by_row, by_row, ids, by_head),
        out_specs=(by_head,) * 4,
        check_vma=False,
    )
```

time: 132 us -> 35.5 us (0.27)
  waiting for transfers between devices: 44 us -> 0 us
  blocking collectives: 36.1 us -> 0 us
  Pallas kernels: 0 us -> 24.5 us
  starting transfers between devices: 15.2 us -> 0 us
  between operations: 14.2 us -> 0.66 us
  matrix products: 7.22 us -> 0 us
  other arithmetic: 2.65 us -> 0 us
    reduce_scatter x2 -> x0, waiting for transfers between devices: 38.1 us -> none  [the longest x1 21.4 us: local(): lax.psum_scatter(value_parts.reshape(seq_len, -1).astype(jnp.bfloat16), '...]
    all_gather x6 -> x0, blocking collectives: 36.1 us -> none  [the longest x1 8.02 us: local(): lax.all_gather(back_value, 'fsdp', axis=0, tiled=True)]
    pallas_call x0 -> x1, Pallas kernels: none -> 24.5 us  [local(): pl.pallas_call(functools.partial(kernel, n_s, n_f, n_t), out_shape=[jax.S...]
    all_to_all x3 -> x0, starting transfers between devices: 11.5 us -> none  [the longest x1 4.78 us: local(): lax.all_to_all(stash_key, 'tp', split_axis=1, concat_axis=0, tiled=True)]
    dot_general x8 -> x0, matrix products: 7.22 us -> none  [the longest x1 2.11 us: block_grads(): jnp.einsum('igrj,igrd->jgd', probabilities.astype(jnp.bfloat16), grad_hea...]
    all_to_all x3 -> x0, waiting for transfers between devices: 5.86 us -> none  [the longest x1 3.34 us: local(): lax.all_to_all(stash_key, 'tp', split_axis=1, concat_axis=0, tiled=True)]
    ppermute x4 -> x0, starting transfers between devices: 3.65 us -> none  [partner(): return lax.ppermute(block, axis, route)]
    unnamed x10 -> x22, local copies, waits for them, and re-layouts: 6.52 us -> 9.82 us
  transfers between devices with their start and end apart: 9 -> 0, of which waited for: 4 -> 0; matrix products, arithmetic and copies ran while one was open for 12% -> 0% of each run, Pallas kernels for 0% -> 0%
where the time goes in v1:
time: 35.5 us; the launch traced here: 35 us
  Pallas kernels  24.5 us (69%)
  local copies, waits for them, and re-layouts  9.82 us (28%)
  between operations  0.66 us (2%)
    pallas_call x1, Pallas kernels, local(): pl.pallas_call(functools.partial(kernel, n_s, n_f, n_t), out_shape=[jax.S...  24.5 us
    unnamed x22, local copies, waits for them, and re-layouts  9.82 us

profile of v1, /device:TPU:1, one launch (start us, length us, event | category | flops | bytes accessed | tf_op | source)
XLA Modules:
  0.0 35.0 jit_solution(12023278441690397724)
XLA Ops:
  0.6 0.0 copy-start
  0.6 0.9 %copy-done = bf16[1,128,1024]{2,1,0:T(8,128)(2,1)S(1)} copy-done((bf16[1,128,1024]{2,1,0:T(8,128)(2,1)S(1)}, bf16[1,128,1024]{2,1,0:T(8,128)(2,1)}, u32[]{:S(2)}) %copy-start) | copy-done | bytes 262168
  1.6 0.0 copy-start.1
  1.6 0.9 %copy-done.1 = bf16[1,32,4096]{2,1,0:T(8,128)(2,1)S(1)} copy-done((bf16[1,32,4096]{2,1,0:T(8,128)(2,1)S(1)}, bf16[1,32,4096]{2,1,0:T(8,128)(2,1)}, u32[]{:S(2)}) %copy-start.1) | copy-done | bytes 262168
  2.5 0.0 copy-start.2
  2.5 0.9 %copy-done.2 = bf16[1,128,1024]{2,1,0:T(8,128)(2,1)S(1)} copy-done((bf16[1,128,1024]{2,1,0:T(8,128)(2,1)S(1)}, bf16[1,128,1024]{2,1,0:T(8,128)(2,1)}, u32[]{:S(2)}) %copy-start.2) | copy-done | bytes 262168
  3.5 0.0 copy-start.3
  3.5 0.8 %copy-done.3 = bf16[1,128,128]{2,1,0:T(8,128)(2,1)S(1)} copy-done((bf16[1,128,128]{2,1,0:T(8,128)(2,1)S(1)}, bf16[1,128,128]{2,1,0:T(8,128)(2,1)}, u32[]{:S(2)}) %copy-start.3) | copy-done | bytes 32792
  4.2 0.0 copy-start.4
  4.2 0.8 %copy-done.4 = bf16[1,128,128]{2,1,0:T(8,128)(2,1)S(1)} copy-done((bf16[1,128,128]{2,1,0:T(8,128)(2,1)S(1)}, bf16[1,128,128]{2,1,0:T(8,128)(2,1)}, u32[]{:S(2)}) %copy-start.4) | copy-done | bytes 32792
  5.0 0.0 copy-start.5
  5.0 0.8 %copy-done.5 = bf16[1,32,512]{2,1,0:T(8,128)(2,1)S(1)} copy-done((bf16[1,32,512]{2,1,0:T(8,128)(2,1)S(1)}, bf16[1,32,512]{2,1,0:T(8,128)(2,1)}, u32[]{:S(2)}) %copy-start.5) | copy-done | bytes 32792
  5.8 0.0 copy-start.6
  5.8 0.8 %copy-done.6 = bf16[1,32,512]{2,1,0:T(8,128)(2,1)S(1)} copy-done((bf16[1,32,512]{2,1,0:T(8,128)(2,1)S(1)}, bf16[1,32,512]{2,1,0:T(8,128)(2,1)}, u32[]{:S(2)}) %copy-start.6) | copy-done | bytes 32792
  6.5 0.0 copy-start.7
  6.5 0.7 %copy-done.7 = s32[1,128]{1,0:T(1,128)S(1)} copy-done((s32[1,128]{1,0:T(1,128)S(1)}, s32[1,128]{1,0:T(1,128)}, u32[]{:S(2)}) %copy-start.7) | copy-done | bytes 536
  7.2 0.0 copy-start.8
  7.2 0.7 %copy-done.8 = s32[1,128]{1,0:T(1,128)S(1)} copy-done((s32[1,128]{1,0:T(1,128)S(1)}, s32[1,128]{1,0:T(1,128)}, u32[]{:S(2)}) %copy-start.8) | copy-done | bytes 536
  7.8 24.5 %tick.1 = (bf16[1,128,1024]{2,1,0:T(8,128)(2,1)S(1)}, bf16[1,128,1024]{2,1,0:T(8,128)(2,1)S(1)}, bf16[1,128,128]{2,1,0:T(8,128)(2,1)S(1)}, bf16[1,128,128]{2,1,0:T(8,128)(2,1)S(1)}) custom-call(bf16[1,128,1024]{2,1,0:T(8,128)(2,1)S(1)} %copy-done, bf16[1,128,128]{2,1,0:T(8,128)(2,1)S(1)} %copy-done.3, bf16[1,128,128]{2,1,0:T(8,128)(2,1)S(1)} %copy-done.4, ...), custom_call_target="tpu_custom_call" | custom-call | flops 939524096 | bytes 1572864 | tf_op jit(solution)/shard_map/tick/pallas_call | solution.py:383
  32.4 0.7 %copy.17 = bf16[1,128,1024]{2,1,0:T(8,128)(2,1)} copy(bf16[1,128,1024]{2,1,0:T(8,128)(2,1)S(1)} %get-tuple-element.8) | data formatting | bytes 524288
  33.1 0.7 %copy.18 = bf16[1,128,1024]{2,1,0:T(8,128)(2,1)} copy(bf16[1,128,1024]{2,1,0:T(8,128)(2,1)S(1)} %get-tuple-element.9) | data formatting | bytes 524288
  33.8 0.6 %copy.19 = bf16[1,128,128]{2,1,0:T(8,128)(2,1)} copy(bf16[1,128,128]{2,1,0:T(8,128)(2,1)S(1)} %get-tuple-element.10) | data formatting | bytes 65536
  34.4 0.6 %copy.20 = bf16[1,128,128]{2,1,0:T(8,128)(2,1)} copy(bf16[1,128,128]{2,1,0:T(8,128)(2,1)S(1)} %get-tuple-element.11) | data formatting | bytes 65536
Async XLA Ops:
  0.6 1.0 %copy-start = (bf16[1,128,1024]{2,1,0:T(8,128)(2,1)S(1)}, bf16[1,128,1024]{2,1,0:T(8,128)(2,1)}, u32[]{:S(2)}) copy-start(bf16[1,128,1024]{2,1,0:T(8,128)(2,1)} %q_ref.1) | copy-start | bytes 786436
  1.6 0.9 %copy-start.1 = (bf16[1,32,4096]{2,1,0:T(8,128)(2,1)S(1)}, bf16[1,32,4096]{2,1,0:T(8,128)(2,1)}, u32[]{:S(2)}) copy-start(bf16[1,32,4096]{2,1,0:T(8,128)(2,1)} %hq_ref.1) | copy-start | bytes 786436
  2.5 0.9 %copy-start.2 = (bf16[1,128,1024]{2,1,0:T(8,128)(2,1)S(1)}, bf16[1,128,1024]{2,1,0:T(8,128)(2,1)}, u32[]{:S(2)}) copy-start(bf16[1,128,1024]{2,1,0:T(8,128)(2,1)} %do_ref.1) | copy-start | bytes 786436
  3.5 0.8 %copy-start.3 = (bf16[1,128,128]{2,1,0:T(8,128)(2,1)S(1)}, bf16[1,128,128]{2,1,0:T(8,128)(2,1)}, u32[]{:S(2)}) copy-start(bf16[1,128,128]{2,1,0:T(8,128)(2,1)} %k_ref.1) | copy-start | bytes 98308
  4.2 0.8 %copy-start.4 = (bf16[1,128,128]{2,1,0:T(8,128)(2,1)S(1)}, bf16[1,128,128]{2,1,0:T(8,128)(2,1)}, u32[]{:S(2)}) copy-start(bf16[1,128,128]{2,1,0:T(8,128)(2,1)} %v_ref.1) | copy-start | bytes 98308
  5.0 0.8 %copy-start.5 = (bf16[1,32,512]{2,1,0:T(8,128)(2,1)S(1)}, bf16[1,32,512]{2,1,0:T(8,128)(2,1)}, u32[]{:S(2)}) copy-start(bf16[1,32,512]{2,1,0:T(8,128)(2,1)} %hk_ref.1) | copy-start | bytes 98308
  5.8 0.8 %copy-start.6 = (bf16[1,32,512]{2,1,0:T(8,128)(2,1)S(1)}, bf16[1,32,512]{2,1,0:T(8,128)(2,1)}, u32[]{:S(2)}) copy-start(bf16[1,32,512]{2,1,0:T(8,128)(2,1)} %hv_ref.1) | copy-start | bytes 98308
  6.5 0.7 %copy-start.7 = (s32[1,128]{1,0:T(1,128)S(1)}, s32[1,128]{1,0:T(1,128)}, u32[]{:S(2)}) copy-start(s32[1,128]{1,0:T(1,128)} %sg_ref.1) | copy-start | bytes 1540
  7.2 0.7 %copy-start.8 = (s32[1,128]{1,0:T(1,128)S(1)}, s32[1,128]{1,0:T(1,128)}, u32[]{:S(2)}) copy-start(s32[1,128]{1,0:T(1,128)} %hs_ref.1) | copy-start | bytes 1540

commit v2 on v1

--- a/solution.py
+++ b/solution.py
@@ -14,6 +14,7 @@
 SCALE = 1.0 / math.sqrt(HEAD_DIM)
 SCALE_LOG2 = SCALE * math.log2(math.e)
 MESH = pl.DeviceIdType.MESH
+VMEM_BYTES = 63 * 1024 * 1024
 
 NT = (((1,), (1,)), ((), ()))
 
@@ -50,8 +51,10 @@
     turned,
     s_buf,
     p_buf,
-    dk_acc,
-    dv_acc,
+    p_low,
+    d_low,
+    q_stack,
+    g_stack,
     part_out,
     part_in,
     o_buf,
@@ -200,7 +203,7 @@
     def make_bias(ids):
         own = ids[f]
         for b in range(n_f):
-            key_ids = jnp.transpose(jnp.broadcast_to(ids[b], (HEAD_DIM, rows)))[:, :1]
+            key_ids = jnp.transpose(jnp.broadcast_to(ids[b], (rows, rows)))
             key_pos = b * rows + lax.broadcasted_iota(jnp.int32, (rows, rows), 0)
             own_pos = f * rows + lax.broadcasted_iota(jnp.int32, (rows, rows), 1)
             seen = (key_pos <= own_pos) & (key_ids == own)
@@ -289,15 +292,17 @@
     for copy in second:
         copy.wait_recv()
     make_bias(sg_held)
-    turn(kv_held, 0)
-    dk_acc[...] = jnp.zeros_like(dk_acc)
-    dv_acc[...] = jnp.zeros_like(dv_acc)
+
+    def columns_of(pair):
+        return pl.ds(pl.multiple_of(pair * (PAIR * rows), PAIR * rows), PAIR * rows)
 
     def backward_pair(pair, carry):
+        grad = stacked(g_buf[:, lanes_of(pair)])
+        g_stack[columns_of(pair), :] = grad
         for step in range(n_t):
             query_copy(pair, step).wait_recv()
         query = stacked(hq_buf[pair])
-        grad = stacked(g_buf[:, lanes_of(pair)])
+        q_stack[columns_of(pair), :] = query
         top = scores_of(kv_held, query)
 
         def middle(b, sums):
@@ -315,29 +320,32 @@
         inverse = 1.0 / total
         delta = along * inverse
 
-        def last(b, query_sum):
+        def last(b, carry):
             probs = s_buf[span(b), :] * inverse
-            score_grad = (probs * (p_buf[span(b), :] - delta)).astype(jnp.bfloat16)
-            dv_acc[span(b), :] += dot(probs.astype(jnp.bfloat16), grad)
-            dk_acc[span(b), :] += dot(score_grad, query)
-            return query_sum + dot(turned[:, span(b)], score_grad)
-
-        query_sum = over_blocks(last, jnp.zeros((HEAD_DIM, PAIR * rows), jnp.float32))
-        dq_buf[:, lanes_of(pair)] = untangled(query_sum * SCALE)
+            score_grad = probs * (p_buf[span(b), :] - delta)
+            p_low[span(b), columns_of(pair)] = probs.astype(jnp.bfloat16)
+            d_low[span(b), columns_of(pair)] = score_grad.astype(jnp.bfloat16)
+            return carry
+
+        over_blocks(last, 0)
         return carry
 
     lax.fori_loop(0, pairs, backward_pair, 0)
-    query_grad_copy = pltpu.make_async_copy(dq_buf, dq_ref.at[0], local_sem.at[1])
-    query_grad_copy.start()
 
     def rows_at(index):
         return pl.ds(pl.multiple_of(index * rows, rows), rows)
+
+    def terms(index):
+        key_part = dot(d_low[rows_at(index), :], q_stack[...])
+        value_part = dot(p_low[rows_at(index), :], g_stack[...])
+        return key_part, value_part
 
     reduce = []
     for step in range(1, n_f):
         to = at_f(step)
-        part_out[step - 1, 0] = dk_acc[rows_at(to), :].astype(jnp.bfloat16)
-        part_out[step - 1, 1] = dv_acc[rows_at(to), :].astype(jnp.bfloat16)
+        key_part, value_part = terms(to)
+        part_out[step - 1, 0] = key_part.astype(jnp.bfloat16)
+        part_out[step - 1, 1] = value_part.astype(jnp.bfloat16)
         copy = remote(
             part_out.at[step - 1],
             part_in.at[step - 1],
@@ -347,8 +355,22 @@
         )
         copy.start()
         reduce.append(copy)
-    key_sum = dk_acc[rows_at(f), :]
-    value_sum = dv_acc[rows_at(f), :]
+
+    turn(kv_held, 0)
+
+    def query_pair(pair, carry):
+        def step(b, query_sum):
+            return query_sum + dot(turned[:, span(b)], d_low[span(b), columns_of(pair)])
+
+        query_sum = over_blocks(step, jnp.zeros((HEAD_DIM, PAIR * rows), jnp.float32))
+        dq_buf[:, lanes_of(pair)] = untangled(query_sum * SCALE)
+        return carry
+
+    lax.fori_loop(0, pairs, query_pair, 0)
+    query_grad_copy = pltpu.make_async_copy(dq_buf, dq_ref.at[0], local_sem.at[1])
+    query_grad_copy.start()
+
+    key_sum, value_sum = terms(f)
     for step in range(1, n_f):
         reduce[step - 1].wait_recv()
         key_sum = key_sum + part_in[step - 1, 0].astype(jnp.float32)
@@ -370,6 +392,18 @@
         copy.wait()
 
 
+def hand_over(*refs):
+    count = len(refs) // 2
+    sems = refs[-1]
+    copies = [
+        pltpu.make_async_copy(refs[i], refs[count + i], sems.at[i]) for i in range(count)
+    ]
+    for copy in copies:
+        copy.start()
+    for copy in copies:
+        copy.wait()
+
+
 def local(sizes, *arrays):
     n_s, n_f, n_t = sizes
     queries, key_rows = arrays[0], arrays[1]
@@ -380,7 +414,7 @@
     dma = pltpu.SemaphoreType.DMA
     anywhere = pl.BlockSpec(memory_space=pl.ANY)
     elements = rows * (width // HEAD_DIM) * seq
-    return pl.pallas_call(
+    results = pl.pallas_call(
         functools.partial(kernel, n_s, n_f, n_t),
         out_shape=[
             jax.ShapeDtypeStruct(queries.shape, low),
@@ -402,8 +436,10 @@
             pltpu.VMEM((HEAD_DIM, seq), low),
             pltpu.VMEM((seq, PAIR * rows), full),
             pltpu.VMEM((seq, PAIR * rows), full),
-            pltpu.VMEM((seq, HEAD_DIM), full),
-            pltpu.VMEM((seq, HEAD_DIM), full),
+            pltpu.VMEM((seq, pairs * PAIR * rows), low),
+            pltpu.VMEM((seq, pairs * PAIR * rows), low),
+            pltpu.VMEM((pairs * PAIR * rows, HEAD_DIM), low),
+            pltpu.VMEM((pairs * PAIR * rows, HEAD_DIM), low),
             pltpu.VMEM((n_f - 1, 2, rows, HEAD_DIM), low),
             pltpu.VMEM((n_f - 1, 2, rows, HEAD_DIM), low),
             pltpu.VMEM((rows, width), low),
@@ -423,7 +459,7 @@
             dma((n_f - 1,)),
         ],
         compiler_params=pltpu.CompilerParams(
-            collective_id=0, has_side_effects=True, vmem_limit_bytes=40 * 1024 * 1024
+            collective_id=0, has_side_effects=True, vmem_limit_bytes=VMEM_BYTES
         ),
         cost_estimate=pl.CostEstimate(
             flops=14 * elements * HEAD_DIM,
@@ -432,6 +468,15 @@
         ),
         name="tick",
     )(*arrays)
+    return pl.pallas_call(
+        hand_over,
+        out_shape=[jax.ShapeDtypeStruct(result.shape, low) for result in results],
+        in_specs=[anywhere] * len(results),
+        out_specs=[anywhere] * len(results),
+        scratch_shapes=[dma((len(results),))],
+        compiler_params=pltpu.CompilerParams(vmem_limit_bytes=VMEM_BYTES),
+        name="hand_over",
+    )(*results)
 
 
 def solution(mesh):

time: 35.5 us -> 43.7 us (1.23)
  Pallas kernels: 24.5 us -> 42.9 us
  local copies, waits for them, and re-layouts: 9.82 us -> 0 us
    pallas_call x0 -> x1, Pallas kernels: none -> 19 us  [local(): pl.pallas_call(hand_over, out_shape=[jax.ShapeDtypeStruct(result.shape, l...]
    unnamed x22 -> x0, local copies, waits for them, and re-layouts: 9.82 us -> none
    pallas_call x1, Pallas kernels: 24.5 us -> 23.9 us  [local(): pl.pallas_call(functools.partial(kernel, n_s, n_f, n_t), out_shape=[jax.S...]
where the time goes in v2:
time: 43.7 us; the launch traced here: 43.6 us
  Pallas kernels  42.9 us (98%)
  between operations  0.64 us (1%)
    pallas_call x1, Pallas kernels, local(): pl.pallas_call(functools.partial(kernel, n_s, n_f, n_t), out_shape=[jax.S...  23.9 us
    pallas_call x1, Pallas kernels, local(): pl.pallas_call(hand_over, out_shape=[jax.ShapeDtypeStruct(result.shape, l...  19 us

profile of v2, /device:TPU:1, one launch (start us, length us, event | category | flops | bytes accessed | tf_op | source)
XLA Modules:
  0.0 43.6 jit_solution(14499605298432144922)
XLA Ops:
  0.6 23.9 %tick.1 = (bf16[1,128,1024]{2,1,0:T(8,128)(2,1)}, bf16[1,128,1024]{2,1,0:T(8,128)(2,1)}, bf16[1,128,128]{2,1,0:T(8,128)(2,1)}, bf16[1,128,128]{2,1,0:T(8,128)(2,1)}) custom-call(bf16[1,128,1024]{2,1,0:T(8,128)(2,1)} %q_ref.1, bf16[1,128,128]{2,1,0:T(8,128)(2,1)} %k_ref.1, bf16[1,128,128]{2,1,0:T(8,128)(2,1)} %v_ref.1, s32[1,128]{1,0:T(1,128)} %sg_ref.1, ...), custom_call_target="tpu_custom_call" | custom-call | flops 939524096 | bytes 1572864 | tf_op jit(solution)/shard_map/tick/pallas_call | solution.py:417
  24.6 19.0 %hand_over.1 = (bf16[1,128,1024]{2,1,0:T(8,128)(2,1)}, bf16[1,128,1024]{2,1,0:T(8,128)(2,1)}, bf16[1,128,128]{2,1,0:T(8,128)(2,1)}, bf16[1,128,128]{2,1,0:T(8,128)(2,1)}) custom-call(bf16[1,128,1024]{2,1,0:T(8,128)(2,1)} %get-tuple-element.8.refs_0_, bf16[1,128,1024]{2,1,0:T(8,128)(2,1)} %get-tuple-element.9.refs_1_, ...), custom_call_target="tpu_custom_call" | custom-call | tf_op jit(solution)/shard_map/hand_over/pallas_call | solution.py:471

commit v3 on v2

--- a/solution.py
+++ b/solution.py
@@ -10,6 +10,7 @@
 
 HEAD_DIM = 128
 PAIR = 2
+LOW = 2
 NEG = -1e30
 SCALE = 1.0 / math.sqrt(HEAD_DIM)
 SCALE_LOG2 = SCALE * math.log2(math.e)
@@ -70,6 +71,10 @@
     two_recv,
     hq_send,
     hq_recv,
+    ids_send,
+    ids_recv,
+    on_send,
+    on_recv,
     red_send,
     red_recv,
 ):
@@ -87,6 +92,19 @@
 
     def at_f(step):
         return lax.rem(f + step, n_f)
+
+    high, low_index = f // LOW, f % LOW
+    n_high = n_f // LOW
+    sibling = high * LOW + (LOW - 1 - low_index)
+
+    def at_high(step):
+        return lax.rem(high + step, n_high) * LOW + low_index
+
+    def from_high(step):
+        return lax.rem(high + n_high - step, n_high) * LOW + low_index
+
+    def beside(index):
+        return index - low_index + (LOW - 1 - low_index)
 
     def at_t(step):
         return lax.rem(t + step, n_t)
@@ -148,17 +166,40 @@
     for copy in first:
         copy.start()
 
+    ids_fwd = [
+        remote(
+            sg_ref,
+            sg_fwd.at[f],
+            ids_send.at[step - 1],
+            ids_recv.at[step - 1],
+            (s, at_f(step), t),
+        )
+        for step in range(1, n_f)
+    ]
     fwd = []
-    for step in range(1, n_f):
-        device = (s, at_f(step), t)
-        at = 3 * (step - 1)
-        for which, src in enumerate((k_ref.at[0], v_ref.at[0], sg_ref)):
-            dst = sg_fwd.at[f] if which == 2 else kv_fwd.at[f, which]
+    for step in range(n_high):
+        device = (s, sibling if step == 0 else at_high(step), t)
+        for which, src in enumerate((k_ref, v_ref)):
+            at = 2 * step + which
             fwd.append(
-                remote(src, dst, fwd_send.at[at + which], fwd_recv.at[at + which], device)
+                remote(
+                    src.at[0], kv_fwd.at[f, which], fwd_send.at[at], fwd_recv.at[at], device
+                )
             )
-    for copy in fwd:
-        copy.start()
+    for copy in fwd[2:] + fwd[:2] + ids_fwd:
+        copy.start()
+
+    def passed_on(kv, send_sem, recv_sem):
+        return [
+            remote(
+                kv.at[from_high(step)],
+                kv.at[from_high(step)],
+                send_sem.at[step - 1],
+                recv_sem.at[step - 1],
+                (s, sibling, t),
+            )
+            for step in range(1, n_high)
+        ]
 
     def query_copy(pair, step):
         to = at_t(step)
@@ -180,24 +221,28 @@
     for copy in first:
         copy.wait_recv()
     second = []
-    for step in range(1, n_f):
-        device = (s, at_f(step), t)
-        at = 2 * (step - 1)
+    for step in range(n_high):
+        device = (s, sibling if step == 0 else at_high(step), t)
         second.append(
-            remote(
-                kv_held.at[f], kv_held.at[f], two_send.at[at], two_recv.at[at], device
-            )
-        )
-        second.append(
-            remote(
-                sg_held.at[f],
-                sg_held.at[f],
-                two_send.at[at + 1],
-                two_recv.at[at + 1],
-                device,
-            )
-        )
-    for copy in second:
+            remote(kv_held.at[f], kv_held.at[f], two_send.at[step], two_recv.at[step], device)
+        )
+    ids_held = [
+        remote(
+            sg_held.at[f],
+            sg_held.at[f],
+            ids_send.at[n_f - 2 + step],
+            ids_recv.at[n_f - 2 + step],
+            (s, at_f(step), t),
+        )
+        for step in range(1, n_f)
+    ]
+    for copy in second[1:] + second[:1] + ids_held:
+        copy.start()
+
+    for copy in fwd[2:]:
+        copy.wait_recv()
+    fwd_on = passed_on(kv_fwd, on_send.at[0], on_recv.at[0])
+    for copy in fwd_on:
         copy.start()
 
     def make_bias(ids):
@@ -259,9 +304,11 @@
 
     for copy in local:
         copy.wait()
-    for copy in fwd:
+    for copy in ids_fwd:
         copy.wait_recv()
     make_bias(sg_fwd)
+    for copy in fwd[:2] + fwd_on:
+        copy.wait_recv()
     turn(kv_fwd, 1)
 
     def forward_pair(pair, carry):
@@ -285,13 +332,21 @@
         o_buf[:, lanes_of(pair)] = untangled(out * (1.0 / total))
         return carry
 
-    lax.fori_loop(0, pairs, forward_pair, 0)
+    lax.fori_loop(0, pairs // 2, forward_pair, 0)
+    for copy in second[1:]:
+        copy.wait_recv()
+    held_on = passed_on(kv_held, on_send.at[1], on_recv.at[1])
+    for copy in held_on:
+        copy.start()
+    lax.fori_loop(pairs // 2, pairs, forward_pair, 0)
     out_copy = pltpu.make_async_copy(o_buf, o_ref.at[0], local_sem.at[0])
     out_copy.start()
 
-    for copy in second:
+    for copy in ids_held:
         copy.wait_recv()
     make_bias(sg_held)
+    for copy in second[:1] + held_on:
+        copy.wait_recv()
 
     def columns_of(pair):
         return pl.ds(pl.multiple_of(pair * (PAIR * rows), PAIR * rows), PAIR * rows)
@@ -340,21 +395,34 @@
         value_part = dot(p_low[rows_at(index), :], g_stack[...])
         return key_part, value_part
 
+    def reduce_copy(at, device):
+        return remote(
+            part_out.at[at], part_in.at[at], red_send.at[at], red_recv.at[at], device
+        )
+
+    def put(at, parts):
+        for which in range(2):
+            part_out[at, which] = parts[which].astype(jnp.bfloat16)
+
+    def taken(at, parts):
+        return [parts[which] + part_in[at, which].astype(jnp.float32) for which in range(2)]
+
+    others = n_high - 1
     reduce = []
-    for step in range(1, n_f):
-        to = at_f(step)
-        key_part, value_part = terms(to)
-        part_out[step - 1, 0] = key_part.astype(jnp.bfloat16)
-        part_out[step - 1, 1] = value_part.astype(jnp.bfloat16)
-        copy = remote(
-            part_out.at[step - 1],
-            part_in.at[step - 1],
-            red_send.at[step - 1],
-            red_recv.at[step - 1],
-            (s, to, t),
-        )
-        copy.start()
-        reduce.append(copy)
+    for step in range(1, n_high):
+        put(step - 1, terms(beside(at_high(step))))
+        reduce.append(reduce_copy(step - 1, (s, sibling, t)))
+        reduce[-1].start()
+    for_others = [terms(at_high(step)) for step in range(1, n_high)]
+    put(2 * others, terms(sibling))
+    reduce_side = reduce_copy(2 * others, (s, sibling, t))
+    reduce_side.start()
+    reduce_across = []
+    for step in range(1, n_high):
+        reduce[step - 1].wait_recv()
+        put(others + step - 1, taken(step - 1, for_others[step - 1]))
+        reduce_across.append(reduce_copy(others + step - 1, (s, at_high(step), t)))
+        reduce_across[-1].start()
 
     turn(kv_held, 0)
 
@@ -370,11 +438,13 @@
     query_grad_copy = pltpu.make_async_copy(dq_buf, dq_ref.at[0], local_sem.at[1])
     query_grad_copy.start()
 
-    key_sum, value_sum = terms(f)
-    for step in range(1, n_f):
-        reduce[step - 1].wait_recv()
-        key_sum = key_sum + part_in[step - 1, 0].astype(jnp.float32)
-        value_sum = value_sum + part_in[step - 1, 1].astype(jnp.float32)
+    sums = terms(f)
+    reduce_side.wait_recv()
+    sums = taken(2 * others, sums)
+    for step in range(1, n_high):
+        reduce_across[step - 1].wait_recv()
+        sums = taken(others + step - 1, sums)
+    key_sum, value_sum = sums
     dk_buf[...] = (key_sum * SCALE).astype(jnp.bfloat16)
     dv_buf[...] = value_sum.astype(jnp.bfloat16)
     last_copies = [
@@ -383,7 +453,10 @@
     ]
     for copy in last_copies:
         copy.start()
-    for copy in first + fwd + second + reduce:
+    for copy in (
+        first + fwd + fwd_on + second + held_on + ids_fwd + ids_held
+        + reduce + reduce_across + [reduce_side]
+    ):
         copy.wait_send()
     for pair in range(pairs):
         for step in range(n_t):
@@ -393,14 +466,17 @@
 
 
 def hand_over(*refs):
-    count = len(refs) // 2
-    sems = refs[-1]
-    copies = [
-        pltpu.make_async_copy(refs[i], refs[count + i], sems.at[i]) for i in range(count)
-    ]
-    for copy in copies:
-        copy.start()
-    for copy in copies:
+    count = (len(refs) - 2) // 3
+    sources, results, held = refs[:count], refs[count : 2 * count], refs[2 * count : 3 * count]
+    in_sem, out_sem = refs[3 * count :]
+    into = [pltpu.make_async_copy(sources[i], held[i], in_sem.at[i]) for i in range(count)]
+    out = [pltpu.make_async_copy(held[i], results[i], out_sem.at[i]) for i in range(count)]
+    for copy in into:
+        copy.start()
+    for i in range(count):
+        into[i].wait()
+        out[i].start()
+    for copy in out:
         copy.wait()
 
 
@@ -447,14 +523,18 @@
             pltpu.VMEM((rows, HEAD_DIM), low),
             pltpu.VMEM((rows, HEAD_DIM), low),
             dma((5,)),
-            dma((3 * (n_f - 1),)),
-            dma((3 * (n_f - 1),)),
+            dma((n_f,)),
+            dma((n_f,)),
             dma((2 * n_t + 1,)),
             dma((2 * n_t + 1,)),
+            dma((n_f // LOW,)),
+            dma((n_f // LOW,)),
+            dma((pairs, n_t)),
+            dma((pairs, n_t)),
             dma((2 * (n_f - 1),)),
             dma((2 * (n_f - 1),)),
-            dma((pairs, n_t)),
-            dma((pairs, n_t)),
+            dma((2, n_f // LOW - 1)),
+            dma((2, n_f // LOW - 1)),
             dma((n_f - 1,)),
             dma((n_f - 1,)),
         ],
@@ -473,7 +553,8 @@
         out_shape=[jax.ShapeDtypeStruct(result.shape, low) for result in results],
         in_specs=[anywhere] * len(results),
         out_specs=[anywhere] * len(results),
-        scratch_shapes=[dma((len(results),))],
+        scratch_shapes=[pltpu.VMEM(result.shape, low) for result in results]
+        + [dma((len(results),)), dma((len(results),))],
         compiler_params=pltpu.CompilerParams(vmem_limit_bytes=VMEM_BYTES),
         name="hand_over",
     )(*results)

time: 43.7 us -> 27.5 us (0.63)
  the two profiles are of different devices: /device:TPU:1 before, /device:TPU:0 now
where the time goes in v3:
time: 27.5 us; the launch traced here: 27.3 us
  Pallas kernels  26.7 us (97%)
  between operations  0.64 us (2%)
    pallas_call x1, Pallas kernels, local(): pl.pallas_call(functools.partial(kernel, n_s, n_f, n_t), out_shape=[jax.S...  24.9 us
    pallas_call x1, Pallas kernels, local(): pl.pallas_call(hand_over, out_shape=[jax.ShapeDtypeStruct(result.shape, l...  1.82 us

profile of v3, /device:TPU:0, one launch (start us, length us, event | category | flops | bytes accessed | tf_op | source)
XLA Modules:
  0.0 27.3 jit_solution(16232702345809025168)
XLA Ops:
  0.6 24.9 %tick.1 = (bf16[1,128,1024]{2,1,0:T(8,128)(2,1)}, bf16[1,128,1024]{2,1,0:T(8,128)(2,1)}, bf16[1,128,128]{2,1,0:T(8,128)(2,1)}, bf16[1,128,128]{2,1,0:T(8,128)(2,1)}) custom-call(bf16[1,128,1024]{2,1,0:T(8,128)(2,1)} %q_ref.1, bf16[1,128,128]{2,1,0:T(8,128)(2,1)} %k_ref.1, bf16[1,128,128]{2,1,0:T(8,128)(2,1)} %v_ref.1, s32[1,128]{1,0:T(1,128)} %sg_ref.1, ...), custom_call_target="tpu_custom_call" | custom-call | flops 939524096 | bytes 1572864 | tf_op jit(solution)/shard_map/tick/pallas_call | solution.py:493
  25.5 1.8 %hand_over.1 = (bf16[1,128,1024]{2,1,0:T(8,128)(2,1)}, bf16[1,128,1024]{2,1,0:T(8,128)(2,1)}, bf16[1,128,128]{2,1,0:T(8,128)(2,1)}, bf16[1,128,128]{2,1,0:T(8,128)(2,1)}) custom-call(bf16[1,128,1024]{2,1,0:T(8,128)(2,1)} %get-tuple-element.8.refs_0_, bf16[1,128,1024]{2,1,0:T(8,128)(2,1)} %get-tuple-element.9.refs_1_, ...), custom_call_target="tpu_custom_call" | custom-call | tf_op jit(solution)/shard_map/hand_over/pallas_call | solution.py:551

commit v4 on v2

--- a/solution.py
+++ b/solution.py
@@ -9,7 +9,7 @@
 from jax.sharding import PartitionSpec as P
 
 HEAD_DIM = 128
-PAIR = 2
+PAIR = 4
 NEG = -1e30
 SCALE = 1.0 / math.sqrt(HEAD_DIM)
 SCALE_LOG2 = SCALE * math.log2(math.e)
@@ -48,7 +48,9 @@
     kv_held,
     sg_held,
     bias,
+    bias_held,
     turned,
+    turned_held,
     s_buf,
     p_buf,
     p_low,
@@ -200,7 +202,7 @@
     for copy in second:
         copy.start()
 
-    def make_bias(ids):
+    def make_bias(ids, bias):
         own = ids[f]
         for b in range(n_f):
             key_ids = jnp.transpose(jnp.broadcast_to(ids[b], (rows, rows)))
@@ -227,7 +229,7 @@
             part = kv[pl.ds(b * per, per), which]
         return part.reshape(block, HEAD_DIM)
 
-    def turn(kv, which):
+    def turn(kv, which, turned):
         for b in range(n_f):
             turned[:, b * rows : (b + 1) * rows] = jnp.transpose(kv[b, which])
 
@@ -236,7 +238,7 @@
             [pair_block[:, h * HEAD_DIM : (h + 1) * HEAD_DIM] for h in range(PAIR)], axis=0
         )
 
-    def scores_of(kv, query):
+    def scores_of(kv, query, bias):
         def step(b, top):
             masked = jnp.concatenate([bias[span(b), :]] * PAIR, axis=1)
             scores = dot(piece(kv, 0, b), query, NT) * SCALE_LOG2 + masked
@@ -261,12 +263,12 @@
         copy.wait()
     for copy in fwd:
         copy.wait_recv()
-    make_bias(sg_fwd)
-    turn(kv_fwd, 1)
+    make_bias(sg_fwd, bias)
+    turn(kv_fwd, 1, turned)
 
     def forward_pair(pair, carry):
         query = stacked(q_buf[:, lanes_of(pair)])
-        top = scores_of(kv_fwd, query)
+        top = scores_of(kv_fwd, query, bias)
 
         def step(b, sums):
             total, out = sums
@@ -285,13 +287,11 @@
         o_buf[:, lanes_of(pair)] = untangled(out * (1.0 / total))
         return carry
 
-    lax.fori_loop(0, pairs, forward_pair, 0)
-    out_copy = pltpu.make_async_copy(o_buf, o_ref.at[0], local_sem.at[0])
-    out_copy.start()
+    lax.fori_loop(0, pairs // 2, forward_pair, 0)
 
     for copy in second:
         copy.wait_recv()
-    make_bias(sg_held)
+    make_bias(sg_held, bias_held)
 
     def columns_of(pair):
         return pl.ds(pl.multiple_of(pair * (PAIR * rows), PAIR * rows), PAIR * rows)
@@ -303,7 +303,7 @@
             query_copy(pair, step).wait_recv()
         query = stacked(hq_buf[pair])
         q_stack[columns_of(pair), :] = query
-        top = scores_of(kv_held, query)
+        top = scores_of(kv_held, query, bias_held)
 
         def middle(b, sums):
             total, along = sums
@@ -356,11 +356,11 @@
         copy.start()
         reduce.append(copy)
 
-    turn(kv_held, 0)
+    turn(kv_held, 0, turned_held)
 
     def query_pair(pair, carry):
         def step(b, query_sum):
-            return query_sum + dot(turned[:, span(b)], d_low[span(b), columns_of(pair)])
+            return query_sum + dot(turned_held[:, span(b)], d_low[span(b), columns_of(pair)])
 
         query_sum = over_blocks(step, jnp.zeros((HEAD_DIM, PAIR * rows), jnp.float32))
         dq_buf[:, lanes_of(pair)] = untangled(query_sum * SCALE)
@@ -369,6 +369,9 @@
     lax.fori_loop(0, pairs, query_pair, 0)
     query_grad_copy = pltpu.make_async_copy(dq_buf, dq_ref.at[0], local_sem.at[1])
     query_grad_copy.start()
+    lax.fori_loop(pairs // 2, pairs, forward_pair, 0)
+    out_copy = pltpu.make_async_copy(o_buf, o_ref.at[0], local_sem.at[0])
+    out_copy.start()
 
     key_sum, value_sum = terms(f)
     for step in range(1, n_f):
@@ -393,14 +396,17 @@
 
 
 def hand_over(*refs):
-    count = len(refs) // 2
-    sems = refs[-1]
-    copies = [
-        pltpu.make_async_copy(refs[i], refs[count + i], sems.at[i]) for i in range(count)
-    ]
-    for copy in copies:
-        copy.start()
-    for copy in copies:
+    count = (len(refs) - 2) // 3
+    sources, results, held = refs[:count], refs[count : 2 * count], refs[2 * count : 3 * count]
+    in_sem, out_sem = refs[3 * count :]
+    into = [pltpu.make_async_copy(sources[i], held[i], in_sem.at[i]) for i in range(count)]
+    out = [pltpu.make_async_copy(held[i], results[i], out_sem.at[i]) for i in range(count)]
+    for copy in into:
+        copy.start()
+    for i in range(count):
+        into[i].wait()
+        out[i].start()
+    for copy in out:
         copy.wait()
 
 
@@ -433,6 +439,8 @@
             pltpu.VMEM((n_f, 2, rows, HEAD_DIM), low),
             pltpu.VMEM((n_f, 1, rows), jnp.int32),
             pltpu.VMEM((seq, rows), full),
+            pltpu.VMEM((seq, rows), full),
+            pltpu.VMEM((HEAD_DIM, seq), low),
             pltpu.VMEM((HEAD_DIM, seq), low),
             pltpu.VMEM((seq, PAIR * rows), full),
             pltpu.VMEM((seq, PAIR * rows), full),
@@ -473,7 +481,8 @@
         out_shape=[jax.ShapeDtypeStruct(result.shape, low) for result in results],
         in_specs=[anywhere] * len(results),
         out_specs=[anywhere] * len(results),
-        scratch_shapes=[dma((len(results),))],
+        scratch_shapes=[pltpu.VMEM(result.shape, low) for result in results]
+        + [dma((len(results),)), dma((len(results),))],
         compiler_params=pltpu.CompilerParams(vmem_limit_bytes=VMEM_BYTES),
         name="hand_over",
     )(*results)

time: 43.7 us -> 26 us (0.59)
  Pallas kernels: 42.9 us -> 25.2 us
    pallas_call x1, Pallas kernels: 19 us -> 1.82 us  [local(): pl.pallas_call(hand_over, out_shape=[jax.ShapeDtypeStruct(result.shape, l...]
    pallas_call x1, Pallas kernels: 23.9 us -> 23.4 us  [local(): pl.pallas_call(functools.partial(kernel, n_s, n_f, n_t), out_shape=[jax.S...]
where the time goes in v4:
time: 26 us; the launch traced here: 25.8 us
  Pallas kernels  25.2 us (97%)
  between operations  0.64 us (2%)
    pallas_call x1, Pallas kernels, local(): pl.pallas_call(functools.partial(kernel, n_s, n_f, n_t), out_shape=[jax.S...  23.4 us
    pallas_call x1, Pallas kernels, local(): pl.pallas_call(hand_over, out_shape=[jax.ShapeDtypeStruct(result.shape, l...  1.82 us

profile of v4, /device:TPU:1, one launch (start us, length us, event | category | flops | bytes accessed | tf_op | source)
XLA Modules:
  0.0 25.8 jit_solution(633196202179917929)
XLA Ops:
  0.6 23.4 %tick.1 = (bf16[1,128,1024]{2,1,0:T(8,128)(2,1)}, bf16[1,128,1024]{2,1,0:T(8,128)(2,1)}, bf16[1,128,128]{2,1,0:T(8,128)(2,1)}, bf16[1,128,128]{2,1,0:T(8,128)(2,1)}) custom-call(bf16[1,128,1024]{2,1,0:T(8,128)(2,1)} %q_ref.1, bf16[1,128,128]{2,1,0:T(8,128)(2,1)} %k_ref.1, bf16[1,128,128]{2,1,0:T(8,128)(2,1)} %v_ref.1, s32[1,128]{1,0:T(1,128)} %sg_ref.1, ...), custom_call_target="tpu_custom_call" | custom-call | flops 939524096 | bytes 1572864 | tf_op jit(solution)/shard_map/tick/pallas_call | solution.py:423
  24.0 1.8 %hand_over.1 = (bf16[1,128,1024]{2,1,0:T(8,128)(2,1)}, bf16[1,128,1024]{2,1,0:T(8,128)(2,1)}, bf16[1,128,128]{2,1,0:T(8,128)(2,1)}, bf16[1,128,128]{2,1,0:T(8,128)(2,1)}) custom-call(bf16[1,128,1024]{2,1,0:T(8,128)(2,1)} %get-tuple-element.8.refs_0_, bf16[1,128,1024]{2,1,0:T(8,128)(2,1)} %get-tuple-element.9.refs_1_, ...), custom_call_target="tpu_custom_call" | custom-call | tf_op jit(solution)/shard_map/hand_over/pallas_call | solution.py:479

commit v5 on v4

--- a/solution.py
+++ b/solution.py
@@ -9,7 +9,8 @@
 from jax.sharding import PartitionSpec as P
 
 HEAD_DIM = 128
-PAIR = 4
+PAIR = 2
+WIDE = 4
 NEG = -1e30
 SCALE = 1.0 / math.sqrt(HEAD_DIM)
 SCALE_LOG2 = SCALE * math.log2(math.e)
@@ -59,10 +60,7 @@
     g_stack,
     part_out,
     part_in,
-    o_buf,
-    dq_buf,
-    dk_buf,
-    dv_buf,
+    sums,
     local_sem,
     fwd_send,
     fwd_recv,
@@ -92,6 +90,14 @@
 
     def at_t(step):
         return lax.rem(t + step, n_t)
+
+    for b in range(n_f):
+
+        @pl.when(f < b)
+        def _(b=b):
+            for kv, ids in ((kv_fwd, sg_fwd), (kv_held, sg_held)):
+                kv[b] = jnp.zeros_like(kv[b])
+                ids[b] = jnp.zeros_like(ids[b])
 
     local = [
         pltpu.make_async_copy(k_ref.at[0], kv_fwd.at[f, 0], local_sem.at[0]),
@@ -150,17 +156,35 @@
     for copy in first:
         copy.start()
 
-    fwd = []
-    for step in range(1, n_f):
-        device = (s, at_f(step), t)
-        at = 3 * (step - 1)
-        for which, src in enumerate((k_ref.at[0], v_ref.at[0], sg_ref)):
-            dst = sg_fwd.at[f] if which == 2 else kv_fwd.at[f, which]
-            fwd.append(
-                remote(src, dst, fwd_send.at[at + which], fwd_recv.at[at + which], device)
+    def fwd_copies(step):
+        return [
+            remote(
+                src,
+                sg_fwd.at[f] if which == 2 else kv_fwd.at[f, which],
+                fwd_send.at[step - 1, which],
+                fwd_recv.at[step - 1, which],
+                (s, at_f(step), t),
             )
-    for copy in fwd:
-        copy.start()
+            for which, src in enumerate((k_ref.at[0], v_ref.at[0], sg_ref))
+        ]
+
+    def send_later(copies_of):
+        for step in range(n_f - 1, 0, -1):
+
+            @pl.when(f + step < n_f)
+            def _(step=step):
+                for copy in copies_of(step):
+                    copy.start()
+
+    def take_earlier(copies_of):
+        for step in range(1, n_f):
+
+            @pl.when(f - step >= 0)
+            def _(step=step):
+                for copy in copies_of(step):
+                    copy.wait_recv()
+
+    send_later(fwd_copies)
 
     def query_copy(pair, step):
         to = at_t(step)
@@ -181,26 +205,19 @@
 
     for copy in first:
         copy.wait_recv()
-    second = []
-    for step in range(1, n_f):
-        device = (s, at_f(step), t)
-        at = 2 * (step - 1)
-        second.append(
+    def held_copies(step):
+        return [
             remote(
-                kv_held.at[f], kv_held.at[f], two_send.at[at], two_recv.at[at], device
+                buffer.at[f],
+                buffer.at[f],
+                two_send.at[step - 1, which],
+                two_recv.at[step - 1, which],
+                (s, at_f(step), t),
             )
-        )
-        second.append(
-            remote(
-                sg_held.at[f],
-                sg_held.at[f],
-                two_send.at[at + 1],
-                two_recv.at[at + 1],
-                device,
-            )
-        )
-    for copy in second:
-        copy.start()
+            for which, buffer in enumerate((kv_held, sg_held))
+        ]
+
+    send_later(held_copies)
 
     def make_bias(ids, bias):
         own = ids[f]
@@ -235,23 +252,27 @@
 
     def stacked(pair_block):
         return jnp.concatenate(
-            [pair_block[:, h * HEAD_DIM : (h + 1) * HEAD_DIM] for h in range(PAIR)], axis=0
+            [
+                pair_block[:, h * HEAD_DIM : (h + 1) * HEAD_DIM]
+                for h in range(pair_block.shape[1] // HEAD_DIM)
+            ],
+            axis=0,
         )
 
     def scores_of(kv, query, bias):
         def step(b, top):
-            masked = jnp.concatenate([bias[span(b), :]] * PAIR, axis=1)
+            masked = jnp.concatenate([bias[span(b), :]] * (query.shape[0] // rows), axis=1)
             scores = dot(piece(kv, 0, b), query, NT) * SCALE_LOG2 + masked
-            s_buf[span(b), :] = scores
+            s_buf[span(b), : query.shape[0]] = scores
             return jnp.maximum(top, jnp.max(scores, axis=0, keepdims=True))
 
-        return over_blocks(step, jnp.full((1, PAIR * rows), NEG, jnp.float32))
+        return over_blocks(step, jnp.full((1, query.shape[0]), NEG, jnp.float32))
 
     def untangled(wide):
         return jnp.concatenate(
             [
                 jnp.transpose(wide[:, h * rows : (h + 1) * rows])
-                for h in range(PAIR)
+                for h in range(wide.shape[1] // rows)
             ],
             axis=1,
         ).astype(jnp.bfloat16)
@@ -261,18 +282,20 @@
 
     for copy in local:
         copy.wait()
-    for copy in fwd:
-        copy.wait_recv()
+    take_earlier(fwd_copies)
     make_bias(sg_fwd, bias)
     turn(kv_fwd, 1, turned)
 
-    def forward_pair(pair, carry):
-        query = stacked(q_buf[:, lanes_of(pair)])
+    def wide_lanes(index):
+        return pl.ds(pl.multiple_of(index * WIDE * HEAD_DIM, WIDE * HEAD_DIM), WIDE * HEAD_DIM)
+
+    def forward_pair(index, carry):
+        query = stacked(q_buf[:, wide_lanes(index)])
         top = scores_of(kv_fwd, query, bias)
 
         def step(b, sums):
             total, out = sums
-            weights = jnp.exp2(s_buf[span(b), :] - top)
+            weights = jnp.exp2(s_buf[span(b), : WIDE * rows] - top)
             total = total + jnp.sum(weights, axis=0, keepdims=True)
             out = out + dot(turned[:, span(b)], weights.astype(jnp.bfloat16))
             return total, out
@@ -280,17 +303,17 @@
         total, out = over_blocks(
             step,
             (
-                jnp.zeros((1, PAIR * rows), jnp.float32),
-                jnp.zeros((HEAD_DIM, PAIR * rows), jnp.float32),
+                jnp.zeros((1, WIDE * rows), jnp.float32),
+                jnp.zeros((HEAD_DIM, WIDE * rows), jnp.float32),
             ),
         )
-        o_buf[:, lanes_of(pair)] = untangled(out * (1.0 / total))
+        o_ref[0, :, wide_lanes(index)] = untangled(out * (1.0 / total))
         return carry
 
-    lax.fori_loop(0, pairs // 2, forward_pair, 0)
-
-    for copy in second:
-        copy.wait_recv()
+    wides = width // (WIDE * HEAD_DIM)
+    lax.fori_loop(0, wides // 2, forward_pair, 0)
+
+    take_earlier(held_copies)
     make_bias(sg_held, bias_held)
 
     def columns_of(pair):
@@ -307,9 +330,9 @@
 
         def middle(b, sums):
             total, along = sums
-            weights = jnp.exp2(s_buf[span(b), :] - top)
+            weights = jnp.exp2(s_buf[span(b), : PAIR * rows] - top)
             prob_grad = dot(piece(kv_held, 1, b), grad, NT)
-            s_buf[span(b), :] = weights
+            s_buf[span(b), : PAIR * rows] = weights
             p_buf[span(b), :] = prob_grad
             total = total + jnp.sum(weights, axis=0, keepdims=True)
             along = along + jnp.sum(weights * prob_grad, axis=0, keepdims=True)
@@ -321,7 +344,7 @@
         delta = along * inverse
 
         def last(b, carry):
-            probs = s_buf[span(b), :] * inverse
+            probs = s_buf[span(b), : PAIR * rows] * inverse
             score_grad = probs * (p_buf[span(b), :] - delta)
             p_low[span(b), columns_of(pair)] = probs.astype(jnp.bfloat16)
             d_low[span(b), columns_of(pair)] = score_grad.astype(jnp.bfloat16)
@@ -340,21 +363,23 @@
         value_part = dot(p_low[rows_at(index), :], g_stack[...])
         return key_part, value_part
 
-    reduce = []
-    for step in range(1, n_f):
-        to = at_f(step)
-        key_part, value_part = terms(to)
-        part_out[step - 1, 0] = key_part.astype(jnp.bfloat16)
-        part_out[step - 1, 1] = value_part.astype(jnp.bfloat16)
-        copy = remote(
+    def reduce_copy(step):
+        return remote(
             part_out.at[step - 1],
             part_in.at[step - 1],
             red_send.at[step - 1],
             red_recv.at[step - 1],
-            (s, to, t),
-        )
-        copy.start()
-        reduce.append(copy)
+            (s, lax.rem(f + n_f - step, n_f), t),
+        )
+
+    for step in range(n_f - 1, 0, -1):
+
+        @pl.when(f - step >= 0)
+        def _(step=step):
+            key_part, value_part = terms(lax.rem(f + n_f - step, n_f))
+            part_out[step - 1, 0] = key_part.astype(jnp.bfloat16)
+            part_out[step - 1, 1] = value_part.astype(jnp.bfloat16)
+            reduce_copy(step).start()
 
     turn(kv_held, 0, turned_held)
 
@@ -363,50 +388,51 @@
             return query_sum + dot(turned_held[:, span(b)], d_low[span(b), columns_of(pair)])
 
         query_sum = over_blocks(step, jnp.zeros((HEAD_DIM, PAIR * rows), jnp.float32))
-        dq_buf[:, lanes_of(pair)] = untangled(query_sum * SCALE)
+        dq_ref[0, :, lanes_of(pair)] = untangled(query_sum * SCALE)
         return carry
 
     lax.fori_loop(0, pairs, query_pair, 0)
-    query_grad_copy = pltpu.make_async_copy(dq_buf, dq_ref.at[0], local_sem.at[1])
-    query_grad_copy.start()
-    lax.fori_loop(pairs // 2, pairs, forward_pair, 0)
-    out_copy = pltpu.make_async_copy(o_buf, o_ref.at[0], local_sem.at[0])
-    out_copy.start()
+    lax.fori_loop(wides // 2, wides, forward_pair, 0)
 
     key_sum, value_sum = terms(f)
+    sums[0] = key_sum
+    sums[1] = value_sum
     for step in range(1, n_f):
-        reduce[step - 1].wait_recv()
-        key_sum = key_sum + part_in[step - 1, 0].astype(jnp.float32)
-        value_sum = value_sum + part_in[step - 1, 1].astype(jnp.float32)
-    dk_buf[...] = (key_sum * SCALE).astype(jnp.bfloat16)
-    dv_buf[...] = value_sum.astype(jnp.bfloat16)
-    last_copies = [
-        pltpu.make_async_copy(dk_buf, dk_ref.at[0], local_sem.at[2]),
-        pltpu.make_async_copy(dv_buf, dv_ref.at[0], local_sem.at[3]),
-    ]
-    for copy in last_copies:
-        copy.start()
-    for copy in first + fwd + second + reduce:
+
+        @pl.when(f + step < n_f)
+        def _(step=step):
+            reduce_copy(step).wait_recv()
+            sums[...] += part_in[step - 1].astype(jnp.float32)
+
+    dk_ref[0] = (sums[0] * SCALE).astype(jnp.bfloat16)
+    dv_ref[0] = sums[1].astype(jnp.bfloat16)
+    for copy in first:
         copy.wait_send()
+    for step in range(1, n_f):
+
+        @pl.when(f + step < n_f)
+        def _(step=step):
+            for copy in fwd_copies(step) + held_copies(step):
+                copy.wait_send()
+
+        @pl.when(f - step >= 0)
+        def _(step=step):
+            reduce_copy(step).wait_send()
+
     for pair in range(pairs):
         for step in range(n_t):
             query_copy(pair, step).wait_send()
-    for copy in [out_copy, query_grad_copy] + last_copies:
-        copy.wait()
 
 
 def hand_over(*refs):
-    count = (len(refs) - 2) // 3
-    sources, results, held = refs[:count], refs[count : 2 * count], refs[2 * count : 3 * count]
-    in_sem, out_sem = refs[3 * count :]
-    into = [pltpu.make_async_copy(sources[i], held[i], in_sem.at[i]) for i in range(count)]
-    out = [pltpu.make_async_copy(held[i], results[i], out_sem.at[i]) for i in range(count)]
-    for copy in into:
+    count = len(refs) // 2
+    sems = refs[-1]
+    copies = [
+        pltpu.make_async_copy(refs[i], refs[count + i], sems.at[i]) for i in range(count)
+    ]
+    for copy in copies:
         copy.start()
-    for i in range(count):
-        into[i].wait()
-        out[i].start()
-    for copy in out:
+    for copy in copies:
         copy.wait()
 
 
@@ -419,17 +445,18 @@
     low, full = jnp.bfloat16, jnp.float32
     dma = pltpu.SemaphoreType.DMA
     anywhere = pl.BlockSpec(memory_space=pl.ANY)
+    inside = pl.BlockSpec(memory_space=pltpu.VMEM)
     elements = rows * (width // HEAD_DIM) * seq
     results = pl.pallas_call(
         functools.partial(kernel, n_s, n_f, n_t),
         out_shape=[
-            jax.ShapeDtypeStruct(queries.shape, low),
-            jax.ShapeDtypeStruct(queries.shape, low),
-            jax.ShapeDtypeStruct(key_rows.shape, low),
-            jax.ShapeDtypeStruct(key_rows.shape, low),
+            pltpu.VMEM(queries.shape, low),
+            pltpu.VMEM(queries.shape, low),
+            pltpu.VMEM(key_rows.shape, low),
+            pltpu.VMEM(key_rows.shape, low),
         ],
         in_specs=[anywhere] * 9,
-        out_specs=[anywhere] * 4,
+        out_specs=[inside] * 4,
         scratch_shapes=[
             pltpu.VMEM((rows, width), low),
             pltpu.VMEM((rows, width), low),
@@ -442,7 +469,7 @@
             pltpu.VMEM((seq, rows), full),
             pltpu.VMEM((HEAD_DIM, seq), low),
             pltpu.VMEM((HEAD_DIM, seq), low),
-            pltpu.VMEM((seq, PAIR * rows), full),
+            pltpu.VMEM((seq, WIDE * rows), full),
             pltpu.VMEM((seq, PAIR * rows), full),
             pltpu.VMEM((seq, pairs * PAIR * rows), low),
             pltpu.VMEM((seq, pairs * PAIR * rows), low),
@@ -450,17 +477,14 @@
             pltpu.VMEM((pairs * PAIR * rows, HEAD_DIM), low),
             pltpu.VMEM((n_f - 1, 2, rows, HEAD_DIM), low),
             pltpu.VMEM((n_f - 1, 2, rows, HEAD_DIM), low),
-            pltpu.VMEM((rows, width), low),
-            pltpu.VMEM((rows, width), low),
-            pltpu.VMEM((rows, HEAD_DIM), low),
-            pltpu.VMEM((rows, HEAD_DIM), low),
+            pltpu.VMEM((2, rows, HEAD_DIM), full),
             dma((5,)),
-            dma((3 * (n_f - 1),)),
-            dma((3 * (n_f - 1),)),
+            dma((n_f - 1, 3)),
+            dma((n_f - 1, 3)),
             dma((2 * n_t + 1,)),
             dma((2 * n_t + 1,)),
-            dma((2 * (n_f - 1),)),
-            dma((2 * (n_f - 1),)),
+            dma((n_f - 1, 2)),
+            dma((n_f - 1, 2)),
             dma((pairs, n_t)),
             dma((pairs, n_t)),
             dma((n_f - 1,)),
@@ -478,12 +502,11 @@
     )(*arrays)
     return pl.pallas_call(
         hand_over,
-        out_shape=[jax.ShapeDtypeStruct(result.shape, low) for result in results],
-        in_specs=[anywhere] * len(results),
+        out_shape=[pltpu.HBM(result.shape, low) for result in results],
+        in_specs=[inside] * len(results),
         out_specs=[anywhere] * len(results),
-        scratch_shapes=[pltpu.VMEM(result.shape, low) for result in results]
-        + [dma((len(results),)), dma((len(results),))],
-        compiler_params=pltpu.CompilerParams(vmem_limit_bytes=VMEM_BYTES),
+        scratch_shapes=[dma((len(results),))],
+        compiler_params=pltpu.CompilerParams(vmem_limit_bytes=VMEM_BYTES // 4),
         name="hand_over",
     )(*results)
 

time: 26 us -> 24.5 us (0.942)
  Pallas kernels: 25.2 us -> 23.7 us
    pallas_call x2, Pallas kernels: 25.2 us -> 23.7 us  [the longest x1 22.9 us: local(): pl.pallas_call(functools.partial(kernel, n_s, n_f, n_t), out_shape=[pltpu...]
where the time goes in v5:
time: 24.5 us; the launch traced here: 24.4 us
  Pallas kernels  23.7 us (97%)
  between operations  0.64 us (3%)
    pallas_call x1, Pallas kernels, local(): pl.pallas_call(functools.partial(kernel, n_s, n_f, n_t), out_shape=[pltpu...  22.9 us
    pallas_call x1, Pallas kernels, local(): pl.pallas_call(hand_over, out_shape=[pltpu.HBM(result.shape, low) for res...  0.84 us

profile of v5, /device:TPU:1, one launch (start us, length us, event | category | flops | bytes accessed | tf_op | source)
XLA Modules:
  0.0 24.4 jit_solution(8647623287616661929)
XLA Ops:
  0.6 22.9 %tick.1 = (bf16[1,128,1024]{2,1,0:T(8,128)(2,1)S(1)}, bf16[1,128,1024]{2,1,0:T(8,128)(2,1)S(1)}, bf16[1,128,128]{2,1,0:T(8,128)(2,1)S(1)}, bf16[1,128,128]{2,1,0:T(8,128)(2,1)S(1)}) custom-call(bf16[1,128,1024]{2,1,0:T(8,128)(2,1)} %q_ref.1, bf16[1,128,128]{2,1,0:T(8,128)(2,1)} %k_ref.1, bf16[1,128,128]{2,1,0:T(8,128)(2,1)} %v_ref.1, s32[1,128]{1,0:T(1,128)} %sg_ref.1, ...), custom_call_target="tpu_custom_call" | custom-call | flops 939524096 | bytes 1572864 | tf_op jit(solution)/shard_map/tick/pallas_call | solution.py:450
  23.6 0.8 %hand_over.1 = (bf16[1,128,1024]{2,1,0:T(8,128)(2,1)}, bf16[1,128,1024]{2,1,0:T(8,128)(2,1)}, bf16[1,128,128]{2,1,0:T(8,128)(2,1)}, bf16[1,128,128]{2,1,0:T(8,128)(2,1)}) custom-call(bf16[1,128,1024]{2,1,0:T(8,128)(2,1)S(1)} %get-tuple-element.8.refs_0_, bf16[1,128,1024]{2,1,0:T(8,128)(2,1)S(1)} %get-tuple-element.9.refs_1_, ...), custom_call_target="tpu_custom_call" | custom-call | tf_op jit(solution)/shard_map/hand_over/pallas_call | solution.py:503

commit v6 on v5

--- a/solution.py
+++ b/solution.py
@@ -10,6 +10,7 @@
 
 HEAD_DIM = 128
 PAIR = 2
+LOW = 2
 WIDE = 4
 NEG = -1e30
 SCALE = 1.0 / math.sqrt(HEAD_DIM)
@@ -66,6 +67,10 @@
     fwd_recv,
     one_send,
     one_recv,
+    ids_send,
+    ids_recv,
+    on_send,
+    on_recv,
     two_send,
     two_recv,
     hq_send,
@@ -87,6 +92,11 @@
 
     def at_f(step):
         return lax.rem(f + step, n_f)
+
+    high = f // LOW
+    lane = f - high * LOW
+    n_high = n_f // LOW
+    sibling = high * LOW + (LOW - 1 - lane)
 
     def at_t(step):
         return lax.rem(t + step, n_t)
@@ -156,16 +166,40 @@
     for copy in first:
         copy.start()
 
-    def fwd_copies(step):
+    def fwd_copies(at, device):
         return [
             remote(
-                src,
-                sg_fwd.at[f] if which == 2 else kv_fwd.at[f, which],
-                fwd_send.at[step - 1, which],
-                fwd_recv.at[step - 1, which],
+                src.at[0],
+                kv_fwd.at[f, which],
+                fwd_send.at[at, which],
+                fwd_recv.at[at, which],
+                (s, device, t),
+            )
+            for which, src in enumerate((k_ref, v_ref))
+        ]
+
+    def across(step):
+        return fwd_copies(step, lax.rem(high + step, n_high) * LOW + lane)
+
+    def passed_on(step):
+        block_at = lax.rem(high + n_high - step, n_high) * LOW + lane
+        return remote(
+            kv_fwd.at[block_at],
+            kv_fwd.at[block_at],
+            on_send.at[step - 1],
+            on_recv.at[step - 1],
+            (s, sibling, t),
+        )
+
+    def fwd_ids(step):
+        return [
+            remote(
+                sg_ref,
+                sg_fwd.at[f],
+                ids_send.at[step - 1],
+                ids_recv.at[step - 1],
                 (s, at_f(step), t),
             )
-            for which, src in enumerate((k_ref.at[0], v_ref.at[0], sg_ref))
         ]
 
     def send_later(copies_of):
@@ -184,7 +218,19 @@
                 for copy in copies_of(step):
                     copy.wait_recv()
 
-    send_later(fwd_copies)
+    for step in range(n_high - 1, 0, -1):
+
+        @pl.when(high + step < n_high)
+        def _(step=step):
+            for copy in across(step):
+                copy.start()
+
+    @pl.when(lane == 0)
+    def _():
+        for copy in fwd_copies(0, sibling):
+            copy.start()
+
+    send_later(fwd_ids)
 
     def query_copy(pair, step):
         to = at_t(step)
@@ -198,10 +244,6 @@
             hq_recv.at[pair, step],
             (mirror, f, to),
         )
-
-    for pair in range(pairs):
-        for step in range(n_t):
-            query_copy(pair, step).start()
 
     for copy in first:
         copy.wait_recv()
@@ -219,6 +261,19 @@
 
     send_later(held_copies)
 
+    for pair in range(pairs):
+        for step in range(n_t):
+            query_copy(pair, step).start()
+
+    for step in range(1, n_high):
+
+        @pl.when(high - step >= 0)
+        def _(step=step):
+            for copy in across(step):
+                copy.wait_recv()
+            passed_on(step).start()
+
+
     def make_bias(ids, bias):
         own = ids[f]
         for b in range(n_f):
@@ -282,8 +337,20 @@
 
     for copy in local:
         copy.wait()
-    take_earlier(fwd_copies)
+    take_earlier(fwd_ids)
     make_bias(sg_fwd, bias)
+
+    @pl.when(lane == LOW - 1)
+    def _():
+        for copy in fwd_copies(0, sibling):
+            copy.wait_recv()
+
+    for step in range(1, n_high):
+
+        @pl.when(high - step >= 0)
+        def _(step=step):
+            passed_on(step).wait_recv()
+
     turn(kv_fwd, 1, turned)
 
     def wide_lanes(index):
@@ -408,11 +475,28 @@
     dv_ref[0] = sums[1].astype(jnp.bfloat16)
     for copy in first:
         copy.wait_send()
+
+    @pl.when(lane == 0)
+    def _():
+        for copy in fwd_copies(0, sibling):
+            copy.wait_send()
+
+    for step in range(1, n_high):
+
+        @pl.when(high + step < n_high)
+        def _(step=step):
+            for copy in across(step):
+                copy.wait_send()
+
+        @pl.when(high - step >= 0)
+        def _(step=step):
+            passed_on(step).wait_send()
+
     for step in range(1, n_f):
 
         @pl.when(f + step < n_f)
         def _(step=step):
-            for copy in fwd_copies(step) + held_copies(step):
+            for copy in fwd_ids(step) + held_copies(step):
                 copy.wait_send()
 
         @pl.when(f - step >= 0)
@@ -479,10 +563,14 @@
             pltpu.VMEM((n_f - 1, 2, rows, HEAD_DIM), low),
             pltpu.VMEM((2, rows, HEAD_DIM), full),
             dma((5,)),
-            dma((n_f - 1, 3)),
-            dma((n_f - 1, 3)),
+            dma((n_f // LOW, 2)),
+            dma((n_f // LOW, 2)),
             dma((2 * n_t + 1,)),
             dma((2 * n_t + 1,)),
+            dma((n_f - 1,)),
+            dma((n_f - 1,)),
+            dma((n_f // LOW - 1,)),
+            dma((n_f // LOW - 1,)),
             dma((n_f - 1, 2)),
             dma((n_f - 1, 2)),
             dma((pairs, n_t)),

time: 24.5 us -> 24.4 us (level)
  no operation moved by 1% of the time
where the time goes in v6:
time: 24.4 us; the launch traced here: 24.3 us
  Pallas kernels  23.6 us (97%)
  between operations  0.64 us (3%)
    pallas_call x1, Pallas kernels, local(): pl.pallas_call(functools.partial(kernel, n_s, n_f, n_t), out_shape=[pltpu...  22.8 us
    pallas_call x1, Pallas kernels, local(): pl.pallas_call(hand_over, out_shape=[pltpu.HBM(result.shape, low) for res...  0.84 us

profile of v6, /device:TPU:1, one launch (start us, length us, event | category | flops | bytes accessed | tf_op | source)
XLA Modules:
  0.0 24.3 jit_solution(15517990345628293575)
XLA Ops:
  0.6 22.8 %tick.1 = (bf16[1,128,1024]{2,1,0:T(8,128)(2,1)S(1)}, bf16[1,128,1024]{2,1,0:T(8,128)(2,1)S(1)}, bf16[1,128,128]{2,1,0:T(8,128)(2,1)S(1)}, bf16[1,128,128]{2,1,0:T(8,128)(2,1)S(1)}) custom-call(bf16[1,128,1024]{2,1,0:T(8,128)(2,1)} %q_ref.1, bf16[1,128,128]{2,1,0:T(8,128)(2,1)} %k_ref.1, bf16[1,128,128]{2,1,0:T(8,128)(2,1)} %v_ref.1, s32[1,128]{1,0:T(1,128)} %sg_ref.1, ...), custom_call_target="tpu_custom_call" | custom-call | flops 939524096 | bytes 1572864 | tf_op jit(solution)/shard_map/tick/pallas_call | solution.py:534
  23.4 0.8 %hand_over.1 = (bf16[1,128,1024]{2,1,0:T(8,128)(2,1)}, bf16[1,128,1024]{2,1,0:T(8,128)(2,1)}, bf16[1,128,128]{2,1,0:T(8,128)(2,1)}, bf16[1,128,128]{2,1,0:T(8,128)(2,1)}) custom-call(bf16[1,128,1024]{2,1,0:T(8,128)(2,1)S(1)} %get-tuple-element.8.refs_0_, bf16[1,128,1024]{2,1,0:T(8,128)(2,1)S(1)} %get-tuple-element.9.refs_1_, ...), custom_call_target="tpu_custom_call" | custom-call | tf_op jit(solution)/shard_map/hand_over/pallas_call | solution.py:591

commit v7 on v6

--- a/solution.py
+++ b/solution.py
@@ -166,6 +166,26 @@
     for copy in first:
         copy.start()
 
+    def query_copy(pair, step):
+        to = at_t(step)
+        columns = pl.ds(
+            pl.multiple_of(to * width + pair * pair_width, pair_width), pair_width
+        )
+        return remote(
+            hq_ref.at[0, :, columns],
+            hq_buf.at[pair, own_rows, :],
+            hq_send.at[pair, step],
+            hq_recv.at[pair, step],
+            (mirror, f, to),
+        )
+
+    def send_queries(begin, end):
+        for pair in range(begin, end):
+            for step in range(n_t):
+                query_copy(pair, step).start()
+
+    send_queries(0, 1)
+
     def fwd_copies(at, device):
         return [
             remote(
@@ -225,25 +245,6 @@
             for copy in across(step):
                 copy.start()
 
-    @pl.when(lane == 0)
-    def _():
-        for copy in fwd_copies(0, sibling):
-            copy.start()
-
-    send_later(fwd_ids)
-
-    def query_copy(pair, step):
-        to = at_t(step)
-        columns = pl.ds(
-            pl.multiple_of(to * width + pair * pair_width, pair_width), pair_width
-        )
-        return remote(
-            hq_ref.at[0, :, columns],
-            hq_buf.at[pair, own_rows, :],
-            hq_send.at[pair, step],
-            hq_recv.at[pair, step],
-            (mirror, f, to),
-        )
 
     for copy in first:
         copy.wait_recv()
@@ -261,9 +262,14 @@
 
     send_later(held_copies)
 
-    for pair in range(pairs):
-        for step in range(n_t):
-            query_copy(pair, step).start()
+    @pl.when(lane == 0)
+    def _():
+        for copy in fwd_copies(0, sibling):
+            copy.start()
+
+    send_later(fwd_ids)
+
+    send_queries(1, 2)
 
     for step in range(1, n_high):
 
@@ -272,6 +278,8 @@
             for copy in across(step):
                 copy.wait_recv()
             passed_on(step).start()
+
+    send_queries(2, pairs)
 
 
     def make_bias(ids, bias):

time: 24.4 us -> 24.1 us (0.988)
  Pallas kernels: 23.6 us -> 23.3 us
    pallas_call x1, Pallas kernels: 22.8 us -> 22.4 us  [local(): pl.pallas_call(functools.partial(kernel, n_s, n_f, n_t), out_shape=[pltpu...]
where the time goes in v7:
time: 24.1 us; the launch traced here: 23.9 us
  Pallas kernels  23.3 us (97%)
  between operations  0.64 us (3%)
    pallas_call x1, Pallas kernels, local(): pl.pallas_call(functools.partial(kernel, n_s, n_f, n_t), out_shape=[pltpu...  22.4 us
    pallas_call x1, Pallas kernels, local(): pl.pallas_call(hand_over, out_shape=[pltpu.HBM(result.shape, low) for res...  0.84 us

profile of v7, /device:TPU:1, one launch (start us, length us, event | category | flops | bytes accessed | tf_op | source)
XLA Modules:
  0.0 23.9 jit_solution(13124412852074445403)
XLA Ops:
  0.6 22.4 %tick.1 = (bf16[1,128,1024]{2,1,0:T(8,128)(2,1)S(1)}, bf16[1,128,1024]{2,1,0:T(8,128)(2,1)S(1)}, bf16[1,128,128]{2,1,0:T(8,128)(2,1)S(1)}, bf16[1,128,128]{2,1,0:T(8,128)(2,1)S(1)}) custom-call(bf16[1,128,1024]{2,1,0:T(8,128)(2,1)} %q_ref.1, bf16[1,128,128]{2,1,0:T(8,128)(2,1)} %k_ref.1, bf16[1,128,128]{2,1,0:T(8,128)(2,1)} %v_ref.1, s32[1,128]{1,0:T(1,128)} %sg_ref.1, ...), custom_call_target="tpu_custom_call" | custom-call | flops 939524096 | bytes 1572864 | tf_op jit(solution)/shard_map/tick/pallas_call | solution.py:542
  23.1 0.8 %hand_over.1 = (bf16[1,128,1024]{2,1,0:T(8,128)(2,1)}, bf16[1,128,1024]{2,1,0:T(8,128)(2,1)}, bf16[1,128,128]{2,1,0:T(8,128)(2,1)}, bf16[1,128,128]{2,1,0:T(8,128)(2,1)}) custom-call(bf16[1,128,1024]{2,1,0:T(8,128)(2,1)S(1)} %get-tuple-element.8.refs_0_, bf16[1,128,1024]{2,1,0:T(8,128)(2,1)S(1)} %get-tuple-element.9.refs_1_, ...), custom_call_target="tpu_custom_call" | custom-call | tf_op jit(solution)/shard_map/hand_over/pallas_call | solution.py:599

commit v8 on v7

--- a/solution.py
+++ b/solution.py
@@ -322,11 +322,11 @@
             axis=0,
         )
 
-    def scores_of(kv, query, bias):
+    def scores_of(kv, query, bias, at=0):
         def step(b, top):
             masked = jnp.concatenate([bias[span(b), :]] * (query.shape[0] // rows), axis=1)
             scores = dot(piece(kv, 0, b), query, NT) * SCALE_LOG2 + masked
-            s_buf[span(b), : query.shape[0]] = scores
+            s_buf[span(b), at : at + query.shape[0]] = scores
             return jnp.maximum(top, jnp.max(scores, axis=0, keepdims=True))
 
         return over_blocks(step, jnp.full((1, query.shape[0]), NEG, jnp.float32))
@@ -341,6 +341,8 @@
         ).astype(jnp.bfloat16)
 
     def lanes_of(pair):
+        if isinstance(pair, int):
+            return pl.ds(pair * pair_width, pair_width)
         return pl.ds(pl.multiple_of(pair * pair_width, pair_width), pair_width)
 
     for copy in local:
@@ -392,23 +394,26 @@
     make_bias(sg_held, bias_held)
 
     def columns_of(pair):
+        if isinstance(pair, int):
+            return pl.ds(pair * PAIR * rows, PAIR * rows)
         return pl.ds(pl.multiple_of(pair * (PAIR * rows), PAIR * rows), PAIR * rows)
 
     def backward_pair(pair, carry):
+        half = pair % (WIDE // PAIR) * (PAIR * rows)
         grad = stacked(g_buf[:, lanes_of(pair)])
         g_stack[columns_of(pair), :] = grad
         for step in range(n_t):
             query_copy(pair, step).wait_recv()
         query = stacked(hq_buf[pair])
         q_stack[columns_of(pair), :] = query
-        top = scores_of(kv_held, query, bias_held)
+        top = scores_of(kv_held, query, bias_held, half)
 
         def middle(b, sums):
             total, along = sums
-            weights = jnp.exp2(s_buf[span(b), : PAIR * rows] - top)
+            weights = jnp.exp2(s_buf[span(b), half : half + PAIR * rows] - top)
             prob_grad = dot(piece(kv_held, 1, b), grad, NT)
-            s_buf[span(b), : PAIR * rows] = weights
-            p_buf[span(b), :] = prob_grad
+            s_buf[span(b), half : half + PAIR * rows] = weights
+            p_buf[span(b), half : half + PAIR * rows] = prob_grad
             total = total + jnp.sum(weights, axis=0, keepdims=True)
             along = along + jnp.sum(weights * prob_grad, axis=0, keepdims=True)
             return total, along
@@ -419,8 +424,8 @@
         delta = along * inverse
 
         def last(b, carry):
-            probs = s_buf[span(b), : PAIR * rows] * inverse
-            score_grad = probs * (p_buf[span(b), :] - delta)
+            probs = s_buf[span(b), half : half + PAIR * rows] * inverse
+            score_grad = probs * (p_buf[span(b), half : half + PAIR * rows] - delta)
             p_low[span(b), columns_of(pair)] = probs.astype(jnp.bfloat16)
             d_low[span(b), columns_of(pair)] = score_grad.astype(jnp.bfloat16)
             return carry
@@ -428,7 +433,8 @@
         over_blocks(last, 0)
         return carry
 
-    lax.fori_loop(0, pairs, backward_pair, 0)
+    for pair in range(pairs):
+        backward_pair(pair, 0)
 
     def rows_at(index):
         return pl.ds(pl.multiple_of(index * rows, rows), rows)
@@ -562,7 +568,7 @@
             pltpu.VMEM((HEAD_DIM, seq), low),
             pltpu.VMEM((HEAD_DIM, seq), low),
             pltpu.VMEM((seq, WIDE * rows), full),
-            pltpu.VMEM((seq, PAIR * rows), full),
+            pltpu.VMEM((seq, WIDE * rows), full),
             pltpu.VMEM((seq, pairs * PAIR * rows), low),
             pltpu.VMEM((seq, pairs * PAIR * rows), low),
             pltpu.VMEM((pairs * PAIR * rows, HEAD_DIM), low),

time: 24.1 us -> 24 us (level)
  no operation moved by 1% of the time
where the time goes in v8:
time: 24 us; the launch traced here: 23.9 us
  Pallas kernels  23.3 us (97%)
  between operations  0.64 us (3%)
    pallas_call x1, Pallas kernels, local(): pl.pallas_call(functools.partial(kernel, n_s, n_f, n_t), out_shape=[pltpu...  22.4 us
    pallas_call x1, Pallas kernels, local(): pl.pallas_call(hand_over, out_shape=[pltpu.HBM(result.shape, low) for res...  0.84 us

profile of v8, /device:TPU:1, one launch (start us, length us, event | category | flops | bytes accessed | tf_op | source)
XLA Modules:
  0.0 23.9 jit_solution(2057703452236139866)
XLA Ops:
  0.6 22.4 %tick.1 = (bf16[1,128,1024]{2,1,0:T(8,128)(2,1)S(1)}, bf16[1,128,1024]{2,1,0:T(8,128)(2,1)S(1)}, bf16[1,128,128]{2,1,0:T(8,128)(2,1)S(1)}, bf16[1,128,128]{2,1,0:T(8,128)(2,1)S(1)}) custom-call(bf16[1,128,1024]{2,1,0:T(8,128)(2,1)} %q_ref.1, bf16[1,128,128]{2,1,0:T(8,128)(2,1)} %k_ref.1, bf16[1,128,128]{2,1,0:T(8,128)(2,1)} %v_ref.1, s32[1,128]{1,0:T(1,128)} %sg_ref.1, ...), custom_call_target="tpu_custom_call" | custom-call | flops 939524096 | bytes 1572864 | tf_op jit(solution)/shard_map/tick/pallas_call | solution.py:548
  23.1 0.8 %hand_over.1 = (bf16[1,128,1024]{2,1,0:T(8,128)(2,1)}, bf16[1,128,1024]{2,1,0:T(8,128)(2,1)}, bf16[1,128,128]{2,1,0:T(8,128)(2,1)}, bf16[1,128,128]{2,1,0:T(8,128)(2,1)}) custom-call(bf16[1,128,1024]{2,1,0:T(8,128)(2,1)S(1)} %get-tuple-element.8.refs_0_, bf16[1,128,1024]{2,1,0:T(8,128)(2,1)S(1)} %get-tuple-element.9.refs_1_, ...), custom_call_target="tpu_custom_call" | custom-call | tf_op jit(solution)/shard_map/hand_over/pallas_call | solution.py:605
